TPU v7x, 32 devices: a whole 2x2x4 slice. The times are simulated.
32 devices in a mesh: island: 4 (over z), fsdp: 8 (over y, x, core).
Axes of the slice: x: 2, y: 2, z: 4, core: 2. Of those that a mesh axis runs over, the one named last changes fastest.
Arguments:
- block_input: bfloat16 [4096, 8192], P(('island', 'fsdp')), may hold values from -170 to 170
- lang_ids: int32 [4096], P(('island', 'fsdp')), may hold values from 0 to 15
- queries: bfloat16 [4096, 4096], P(('island', 'fsdp')), may hold values from -52 to 52
- saved_keys: bfloat16 [4096, 512], P(('island', 'fsdp')), may hold values from -4 to 4
- out_grad: bfloat16 [4096, 4096], P(('island', 'fsdp')), may hold values from -70 to 70
- local_wv: bfloat16 [4, 8192, 512], P('island', 'fsdp'), may hold values from -8 to 8
- local_gain: bfloat16 [4, 16, 8192], P('island'), may hold values from -3 to 5
- outer_wv: float32 [8192, 512], P('fsdp', 'island'), may hold values from -4 to 4
- wv_momentum: float32 [8192, 512], P('fsdp', 'island'), may hold values from -1.8 to 1.8
- outer_gain: float32 [16, 8192], P('island', 'fsdp'), may hold values from 0.5 to 1.5
- gain_momentum: float32 [16, 8192], P('island', 'fsdp'), may hold values from -1.8 to 1.8
Outputs:
- new_outer_wv: float32 [8192, 512], P('fsdp', 'island')
- new_wv_momentum: float32 [8192, 512], P('fsdp', 'island')
- new_outer_gain: float32 [16, 8192], P('island', 'fsdp')
- new_gain_momentum: float32 [16, 8192], P('island', 'fsdp')
All inputs are finite; a program needn't handle non-finite values.
Results may differ from a plain program's by a relative error of at most 0.00045.
Values may be sent and summed in bfloat16 or wider, within the bound.
A program may use at most 64 MiB of HBM per device.

v0:
```python
import jax
import jax.numpy as jnp
from jax import lax
from jax.sharding import PartitionSpec as P

HEADS = 32
KV_HEADS = 4
HEAD_DIM = 128


EPSILON = 1e-05
MOMENTUM = 0.9
OUTER_RATE = 0.7
CLIP_SHARE = 0.25


def normalize(input_rows):
    widened = input_rows.astype(jnp.float32)
    average = jnp.mean(widened, axis=-1, keepdims=True)
    centered = widened - average
    variance = jnp.mean(centered * centered, axis=-1, keepdims=True)
    return centered * lax.rsqrt(variance + EPSILON)


def value_grad(query_rows, key_block, grad_rows):
    length = query_rows.shape[0]
    group = HEADS // KV_HEADS
    query_four = query_rows.reshape(length, KV_HEADS, group, HEAD_DIM)
    key_three = key_block.reshape(length, KV_HEADS, HEAD_DIM)
    scores = jnp.einsum(
        "tkgd,skd->kgts", query_four, key_three, preferred_element_type=jnp.float32
    ) * HEAD_DIM ** (-0.5)
    position = jnp.arange(length, dtype=jnp.int32)
    causal = position[:, None] >= position[None, :]
    scores = jnp.where(causal, scores, -jnp.inf)
    row_top = jnp.max(scores, axis=-1, keepdims=True)
    exponent = jnp.exp(scores - row_top)
    weights_bf = (exponent / jnp.sum(exponent, axis=-1, keepdims=True)).astype(jnp.bfloat16)
    grad_four = grad_rows.reshape(length, KV_HEADS, group, HEAD_DIM)
    values = jnp.einsum("kgts,tkgd->skd", weights_bf, grad_four, preferred_element_type=jnp.float32)
    return values.reshape(length, KV_HEADS * HEAD_DIM).astype(jnp.bfloat16)


def body(
    block_input,
    lang_ids,
    queries,
    saved_keys,
    out_grad,
    local_wv,
    local_gain,
    outer_wv,
    wv_momentum,
    outer_gain,
    gain_momentum,
):
    width = block_input.shape[1]
    fsdp_count = lax.axis_size("fsdp")
    island_count = lax.axis_size("island")
    col_block = width // fsdp_count
    kv_width = local_wv.shape[2]
    lang_count = local_gain.shape[1]
    weight_scale = width ** (-0.5)
    col_begin = lax.axis_index("fsdp") * col_block
    standard = normalize(block_input)
    lang_table = lang_ids[None, :] == jnp.arange(lang_count, dtype=jnp.int32)[:, None]
    gain_rows = jnp.dot(
        lang_table.astype(jnp.bfloat16).T, local_gain[0], preferred_element_type=jnp.float32
    )
    normed = (standard * gain_rows).astype(jnp.bfloat16)
    values_grad = value_grad(queries, saved_keys, out_grad)
    weight_rows = local_wv[0]
    col_normed = lax.all_to_all(normed, "fsdp", split_axis=1, concat_axis=0, tiled=True)
    input_grad = (
        jnp.dot(
            values_grad,
            lax.all_gather(weight_rows, "fsdp", axis=0, tiled=True).T,
            preferred_element_type=jnp.float32,
        )
        * weight_scale
    )
    gain_part = jnp.dot(
        lang_table.astype(jnp.float32), standard * input_grad, precision=lax.Precision.HIGHEST
    )
    gain_grad = lax.psum(gain_part, "fsdp")
    wv_grad = (
        jnp.dot(
            col_normed.T,
            lax.all_gather(values_grad, "fsdp", axis=0, tiled=True),
            preferred_element_type=jnp.float32,
        )
        * weight_scale
    )
    wv_square = jnp.sum(wv_grad * wv_grad)
    weight_square = lax.psum(wv_square, "fsdp")
    gain_square = jnp.sum(gain_grad * gain_grad)
    own_grad = lax.dynamic_slice_in_dim(gain_grad, col_begin, col_block, 1)
    wv_clip = jnp.minimum(1.0, CLIP_SHARE * (width * kv_width) ** 0.5 / jnp.sqrt(weight_square))
    gain_clip = jnp.minimum(1.0, CLIP_SHARE * (lang_count * width) ** 0.5 / jnp.sqrt(gain_square))
    new_wv = weight_rows.astype(jnp.float32) - wv_clip * wv_grad
    own_gain = lax.dynamic_slice_in_dim(local_gain[0], col_begin, col_block, 1).astype(jnp.float32)
    new_gain = own_gain - gain_clip * own_grad
    wv_share = kv_width // island_count
    gain_share = lang_count // island_count
    total_wv, total_gain = lax.psum((new_wv, new_gain), "island")
    island_at = lax.axis_index("island")
    total_wv = lax.dynamic_slice_in_dim(total_wv, island_at * wv_share, wv_share, 1)
    total_gain = lax.dynamic_slice_in_dim(total_gain, island_at * gain_share, gain_share, 0)
    delta_wv = outer_wv - total_wv / island_count
    momentum_wv = MOMENTUM * wv_momentum + delta_wv
    result_wv = outer_wv - OUTER_RATE * (delta_wv + MOMENTUM * momentum_wv)
    delta_gain = outer_gain - total_gain / island_count
    momentum_gain = MOMENTUM * gain_momentum + delta_gain
    result_gain = outer_gain - OUTER_RATE * (delta_gain + MOMENTUM * momentum_gain)
    return (result_wv, momentum_wv, result_gain, momentum_gain)


def solution(mesh):
    in_specs = (
        P(("island", "fsdp"), None),
        P(("island", "fsdp")),
        P(("island", "fsdp"), None),
        P(("island", "fsdp"), None),
        P(("island", "fsdp"), None),
        P("island", "fsdp", None),
        P("island", None, None),
        P("fsdp", "island"),
        P("fsdp", "island"),
        P("island", "fsdp"),
        P("island", "fsdp"),
    )
    out_specs = (P("fsdp", "island"), P("fsdp", "island"), P("island", "fsdp"), P("island", "fsdp"))
    return jax.shard_map(body, mesh=mesh, in_specs=in_specs, out_specs=out_specs, check_vma=False)
```

profile of v0, /device:TPU:0, one launch (start us, length us, event | category | flops | bytes accessed | tf_op | source)
XLA Modules:
  0.0 276.3 jit_solution(17101696407753257058)
XLA Ops:
  7.3 1.5 copy.31
  8.9 0.7 copy.29
  9.5 2.3 fusion.33
  11.8 2.8 %fusion.8 = bf16[4,128,128]{1,2,0:T(8,128)(2,1)} fusion(bf16[128,4,8,128]{0,3,2,1:T(8,128)(2,1)S(1)} %bitcast.47, f32[4,8,128,128]{2,3,1,0:T(8,128)} %get-tuple-element.11, f32[4,8,128]{2,1,0:T(8,128)S(1)} %get-tuple-element.10), kind=kOutput, calls=%fused_computation.19 | convolution fusion | flops 135331840 | bytes 3293184 | tf_op jit(solution)/shard_map/kgts,tkgd->skd/dot_general | solution.py:40
  14.7 0.7 all-gather.6.cloned.1.call-update
  15.5 0.4 convert_reduce_fusion
  15.8 0.7 fusion.6
  16.6 0.8 fusion.2
  17.4 1.5 copy.53
  18.9 5.2 %all-to-all-start = ((bf16[128,8,1024]{2,0,1:T(8,128)(2,1)}), bf16[128,8,1024]{2,0,1:T(8,128)(2,1)}, u32[]{:S(2)}, u32[]{:S(2)}) async-start(bf16[128,8,1024]{2,0,1:T(8,128)(2,1)} %bitcast.44), calls=%async_computation | async-start | bytes 4194304 | tf_op jit(solution)/shard_map/all_to_all | solution.py:73
  24.1 30.9 %all-to-all-done = bf16[128,8,1024]{2,0,1:T(8,128)(2,1)} async-done(((bf16[128,8,1024]{2,0,1:T(8,128)(2,1)}), bf16[128,8,1024]{2,0,1:T(8,128)(2,1)}, u32[]{:S(2)}, u32[]{:S(2)}) %all-to-all-start) | async-done | bytes 2097184 | tf_op jit(solution)/shard_map/all_to_all | solution.py:73
  55.1 5.3 %multiply_reduce_fusion = (f32[]{:T(128)}, f32[1024,512]{1,0:T(8,128)}) fusion(bf16[1024,1024]{1,0:T(8,128)(2,1)} %bitcast.3, bf16[1024,512]{0,1:T(8,128)(2,1)} %all-gather.4.cloned.1.call-done), kind=kOutput, calls=%fused_computation.14 | convolution fusion | flops 1075314688 | bytes 5242884 | tf_op jit(solution)/shard_map/dot_general | solution.py:87
  60.3 12.7 %psum.28 = f32[]{:T(128)} all-reduce(f32[]{:T(128)} %get-tuple-element.12), channel_id=1, replica_groups=mesh['island'=4,'fsdp'=8] {'fsdp'}, use_global_device_ids=true, to_apply=%region_5.6 | all-reduce | flops 1 | bytes 8 | tf_op jit(solution)/shard_map/psum | solution.py:95
  73.8 36.0 %all-gather.6.cloned.1.call-done = bf16[1,8192,512]{2,1,0:T(8,128)(2,1)} async-done(((bf16[1,1024,512]{2,1,0:T(8,128)(2,1)}), bf16[1,8192,512]{2,1,0:T(8,128)(2,1)}) %all-gather.6.cloned.1.call-update) | async-done | bytes 8388624 | tf_op jit(solution)/shard_map/all_gather | solution.py:77
  109.7 6.6 %fusion.1 = f32[128,8192]{1,0:T(8,128)S(1)} fusion(bf16[128,512]{0,1:T(8,128)(2,1)S(1)} %bitcast.50, bf16[1,8192,512]{2,1,0:T(8,128)(2,1)} %all-gather.6.cloned.1.call-done, bf16[128,8192]{1,0:T(8,128)(2,1)S(1)} %copy-done, f32[128]{0:T(128)S(1)} %add_rsqrt_fusion, f32[128]{0:T(128)S(1)} %broadcast_multiply_fusion), kind=kOutput, calls=%fused_computation.2 | convolution fusion | flops 1078984704 | bytes 14812160 | tf_op jit(solution)/shard_map/dot_general | solution.py:75
  116.3 2.3 fusion.24
  118.6 0.0 all-reduce.6.cloned.1.call-start
  118.7 1.7 convert_subtract_fusion.1
  120.4 52.9 %all-reduce.4.cloned.1.call-done = f32[16,8192]{1,0:T(8,128)} async-done(((f32[16,8192]{1,0:T(8,128)}), f32[16,8192]{1,0:T(8,128)}) %all-reduce.4.cloned.1.call-update) | async-done | bytes 524304 | tf_op jit(solution)/shard_map/psum | solution.py:85
  173.3 1.8 multiply_reduce_fusion.1
  175.8 1.5 convert_subtract_fusion.2
  177.3 89.0 %all-reduce.6.cloned.1.call-done = (f32[1024,512]{1,0:T(8,128)}, f32[16,1024]{1,0:T(8,128)}) async-done(((f32[1024,512]{1,0:T(8,128)}, f32[16,1024]{1,0:T(8,128)}), (f32[1024,512]{1,0:T(8,128)}, f32[16,1024]{1,0:T(8,128)})) %all-reduce.6.cloned.1.call-update) | async-done | bytes 2162704 | tf_op jit(solution)/shard_map/psum | solution.py:105
  266.3 2.1 multiply_subtract_fusion
  268.4 1.4 multiply_subtract_fusion.2
  (35 shorter events, 0.3 us)
Async XLA Ops:
  7.2 1.6 copy-start.7
  7.2 1.7 copy-start.3
  7.2 47.9 %all-gather.4.cloned.1.call-start = ((), (), s32[]{:S(2)}) async-start(), calls=%async_computation.1 | async-start | bytes 1179648 | tf_op jit(solution)/shard_map/all_gather | solution.py:89
  11.8 3.6 %copy-start = (bf16[128,8192]{1,0:T(8,128)(2,1)S(1)}, bf16[128,8192]{1,0:T(8,128)(2,1)}, u32[]{:S(2)}) copy-start(bf16[128,8192]{1,0:T(8,128)(2,1)} %param.11) | copy-start | bytes 6291460
  14.7 95.0 %all-gather.6.cloned.1.call-start = ((), (), s32[]{:S(2)}) async-start(), calls=%async_computation.3 | async-start | bytes 9437184 | tf_op jit(solution)/shard_map/all_gather | solution.py:77
  15.4 1.1 copy-start.10
  15.5 1.1 copy-start.11
  18.9 36.1 %all-to-all-start = ((bf16[128,8,1024]{2,0,1:T(8,128)(2,1)}), bf16[128,8,1024]{2,0,1:T(8,128)(2,1)}, u32[]{:S(2)}, u32[]{:S(2)}) async-start(bf16[128,8,1024]{2,0,1:T(8,128)(2,1)} %bitcast.44), calls=%async_computation | async-start | bytes 4194304 | tf_op jit(solution)/shard_map/all_to_all | solution.py:73
  24.1 149.2 %all-reduce.4.cloned.1.call-start = ((), (), s32[]{:S(2)}) async-start(), calls=%async_computation.2 | async-start | bytes 1048576 | tf_op jit(solution)/shard_map/psum | solution.py:85
  55.1 54.7 %copy-start.4 = (bf16[4,128,128]{1,2,0:T(8,128)(2,1)S(1)}, bf16[4,128,128]{1,2,0:T(8,128)(2,1)}, u32[]{:S(2)}) copy-start(bf16[4,128,128]{1,2,0:T(8,128)(2,1)} %fusion.8) | copy-start | bytes 393220
  116.3 2.4 copy-start.1
  116.3 2.4 copy-start.2
  118.6 147.6 %all-reduce.6.cloned.1.call-start = ((), (), s32[]{:S(2)}) async-start(), calls=%async_computation.4 | async-start | bytes 4325376 | tf_op jit(solution)/shard_map/psum | solution.py:105
  120.4 145.9 %copy-start.5 = (f32[1024,128]{1,0:T(8,128)S(1)}, f32[1024,128]{1,0:T(8,128)}, u32[]{:S(2)}) copy-start(f32[1024,128]{1,0:T(8,128)} %param.18) | copy-start | bytes 1572868
  120.4 145.9 %copy-start.6 = (f32[1024,128]{1,0:T(8,128)S(1)}, f32[1024,128]{1,0:T(8,128)}, u32[]{:S(2)}) copy-start(f32[1024,128]{1,0:T(8,128)} %param.19) | copy-start | bytes 1572868
  177.3 91.1 %copy-start.8 = (f32[4,1024]{1,0:T(4,128)S(1)}, f32[4,1024]{1,0:T(4,128)}, u32[]{:S(2)}) copy-start(f32[4,1024]{1,0:T(4,128)} %param.20) | copy-start | bytes 49156
  177.3 91.1 %copy-start.9 = (f32[4,1024]{1,0:T(4,128)S(1)}, f32[4,1024]{1,0:T(4,128)}, u32[]{:S(2)}) copy-start(f32[4,1024]{1,0:T(4,128)} %param.21) | copy-start | bytes 49156
Sparse Core Ops, SparseCore 0:
  14.8 36.0 all-gather.3
  52.8 56.8 all-gather.5
  118.7 54.5 all-reduce.3
  177.4 88.7 all-reduce.5
where the time goes:
time: 277 us; the launch traced here: 276 us
  waiting for transfers between devices  210 us (76%)
  matrix products  20.1 us (7%)
  between operations  15.3 us (6%)
  blocking collectives  12.7 us (5%)
  other arithmetic  9.57 us (3%)
  starting transfers between devices  5.33 us (2%)
  local copies, waits for them, and re-layouts  3.82 us (1%)
    psum x1, waiting for transfers between devices, body(): total_wv, total_gain = lax.psum((new_wv, new_gain), 'island')  89 us
    psum x1, waiting for transfers between devices, body(): gain_grad = lax.psum(gain_part, 'fsdp')  52.9 us
    all_gather x1, waiting for transfers between devices, body(): lax.all_gather(weight_rows, 'fsdp', axis=0, tiled=True)  36 us
    all_to_all x1, waiting for transfers between devices, body(): lax.all_to_all(normed, 'fsdp', split_axis=1, concat_axis=0, tiled=True)  30.9 us
    psum x1, blocking collectives, body(): weight_square = lax.psum(wv_square, 'fsdp')  12.7 us
    dot_general x1, matrix products, body(): jnp.dot(values_grad, lax.all_gather(weight_rows, 'fsdp', axis=0, tiled=Tr...  6.58 us
  transfers between devices with their start and end apart: 5, of which 4 were waited for; matrix products, arithmetic and copies ran while one was open for 4% of the time, Pallas kernels for 0%

commit v1 on v0

--- a/solution.py
+++ b/solution.py
@@ -12,14 +12,6 @@
 MOMENTUM = 0.9
 OUTER_RATE = 0.7
 CLIP_SHARE = 0.25
-
-
-def normalize(input_rows):
-    widened = input_rows.astype(jnp.float32)
-    average = jnp.mean(widened, axis=-1, keepdims=True)
-    centered = widened - average
-    variance = jnp.mean(centered * centered, axis=-1, keepdims=True)
-    return centered * lax.rsqrt(variance + EPSILON)
 
 
 def value_grad(query_rows, key_block, grad_rows):
@@ -62,50 +54,38 @@
     lang_count = local_gain.shape[1]
     weight_scale = width ** (-0.5)
     col_begin = lax.axis_index("fsdp") * col_block
-    standard = normalize(block_input)
-    lang_table = lang_ids[None, :] == jnp.arange(lang_count, dtype=jnp.int32)[:, None]
+    cols = lax.all_to_all(block_input, "fsdp", split_axis=1, concat_axis=0, tiled=True)
+    values_all = lax.all_gather(
+        value_grad(queries, saved_keys, out_grad), "fsdp", axis=0, tiled=True
+    )
+    widened = block_input.astype(jnp.float32)
+    average = jnp.mean(widened, axis=-1, keepdims=True)
+    centered = widened - average
+    variance = jnp.mean(centered * centered, axis=-1, keepdims=True)
+    rows = jnp.concatenate(
+        [average, lax.rsqrt(variance + EPSILON), lang_ids[:, None].astype(jnp.float32)], axis=1
+    )
+    rows_all = lax.all_gather(rows, "fsdp", axis=0, tiled=True)
+    standard = (cols.astype(jnp.float32) - rows_all[:, 0:1]) * rows_all[:, 1:2]
+    lang_table = rows_all[:, 2][None, :] == jnp.arange(lang_count, dtype=jnp.float32)[:, None]
+    own_gain = lax.dynamic_slice_in_dim(local_gain[0], col_begin, col_block, 1)
     gain_rows = jnp.dot(
-        lang_table.astype(jnp.bfloat16).T, local_gain[0], preferred_element_type=jnp.float32
+        lang_table.astype(jnp.bfloat16).T, own_gain, preferred_element_type=jnp.float32
     )
     normed = (standard * gain_rows).astype(jnp.bfloat16)
-    values_grad = value_grad(queries, saved_keys, out_grad)
     weight_rows = local_wv[0]
-    col_normed = lax.all_to_all(normed, "fsdp", split_axis=1, concat_axis=0, tiled=True)
-    input_grad = (
-        jnp.dot(
-            values_grad,
-            lax.all_gather(weight_rows, "fsdp", axis=0, tiled=True).T,
-            preferred_element_type=jnp.float32,
-        )
-        * weight_scale
-    )
-    gain_part = jnp.dot(
+    wv_grad = jnp.dot(normed.T, values_all, preferred_element_type=jnp.float32) * weight_scale
+    input_grad = jnp.dot(values_all, weight_rows.T, preferred_element_type=jnp.float32) * weight_scale
+    own_grad = jnp.dot(
         lang_table.astype(jnp.float32), standard * input_grad, precision=lax.Precision.HIGHEST
     )
-    gain_grad = lax.psum(gain_part, "fsdp")
-    wv_grad = (
-        jnp.dot(
-            col_normed.T,
-            lax.all_gather(values_grad, "fsdp", axis=0, tiled=True),
-            preferred_element_type=jnp.float32,
-        )
-        * weight_scale
-    )
-    wv_square = jnp.sum(wv_grad * wv_grad)
-    weight_square = lax.psum(wv_square, "fsdp")
-    gain_square = jnp.sum(gain_grad * gain_grad)
-    own_grad = lax.dynamic_slice_in_dim(gain_grad, col_begin, col_block, 1)
-    wv_clip = jnp.minimum(1.0, CLIP_SHARE * (width * kv_width) ** 0.5 / jnp.sqrt(weight_square))
-    gain_clip = jnp.minimum(1.0, CLIP_SHARE * (lang_count * width) ** 0.5 / jnp.sqrt(gain_square))
+    squares = lax.psum(jnp.stack([jnp.sum(wv_grad * wv_grad), jnp.sum(own_grad * own_grad)]), "fsdp")
+    wv_clip = jnp.minimum(1.0, CLIP_SHARE * (width * kv_width) ** 0.5 / jnp.sqrt(squares[0]))
+    gain_clip = jnp.minimum(1.0, CLIP_SHARE * (lang_count * width) ** 0.5 / jnp.sqrt(squares[1]))
     new_wv = weight_rows.astype(jnp.float32) - wv_clip * wv_grad
-    own_gain = lax.dynamic_slice_in_dim(local_gain[0], col_begin, col_block, 1).astype(jnp.float32)
-    new_gain = own_gain - gain_clip * own_grad
-    wv_share = kv_width // island_count
-    gain_share = lang_count // island_count
-    total_wv, total_gain = lax.psum((new_wv, new_gain), "island")
-    island_at = lax.axis_index("island")
-    total_wv = lax.dynamic_slice_in_dim(total_wv, island_at * wv_share, wv_share, 1)
-    total_gain = lax.dynamic_slice_in_dim(total_gain, island_at * gain_share, gain_share, 0)
+    new_gain = own_gain.astype(jnp.float32) - gain_clip * own_grad
+    total_wv = lax.psum_scatter(new_wv, "island", scatter_dimension=1, tiled=True)
+    total_gain = lax.psum_scatter(new_gain, "island", scatter_dimension=0, tiled=True)
     delta_wv = outer_wv - total_wv / island_count
     momentum_wv = MOMENTUM * wv_momentum + delta_wv
     result_wv = outer_wv - OUTER_RATE * (delta_wv + MOMENTUM * momentum_wv)

time: 277 us -> 178 us (0.64)
  waiting for transfers between devices: 210 us -> 75.2 us
  blocking collectives: 12.7 us -> 35.4 us
  local copies, waits for them, and re-layouts: 3.82 us -> 13.8 us
  other arithmetic: 9.57 us -> 15.3 us
  matrix products: 20.1 us -> 16.9 us
    psum x2 -> x0, waiting for transfers between devices: 142 us -> none  [the longest x1 89 us: body(): total_wv, total_gain = lax.psum((new_wv, new_gain), 'island')]
    reduce_scatter x0 -> x1, waiting for transfers between devices: none -> 44.6 us  [body(): lax.psum_scatter(new_wv, 'island', scatter_dimension=1, tiled=True)]
    all_gather x2 -> x1, waiting for transfers between devices: 36 us -> 0.01 us  [body(): lax.all_gather(value_grad(queries, saved_keys, out_grad), 'fsdp', axis=0,...]
    all_to_all x1, waiting for transfers between devices: 30.9 us -> 0.01 us  [body(): lax.all_to_all(block_input, 'fsdp', split_axis=1, concat_axis=0, tiled=True)]
    unnamed x4, waiting for transfers between devices: 0.74 us -> 30.5 us
    all_gather x0 -> x1, blocking collectives: none -> 22.2 us  [body(): rows_all = lax.all_gather(rows, 'fsdp', axis=0, tiled=True)]
    unnamed x25 -> x35, local copies, waits for them, and re-layouts: 1.58 us -> 7.09 us
    convert_element_type x0 -> x1, local copies, waits for them, and re-layouts: none -> 5.38 us  [body(): standard = (cols.astype(jnp.float32) - rows_all[:, 0:1]) * rows_all[:, 1:2]]
  transfers between devices with their start and end apart: 5 -> 4, of which waited for: 4 -> 2; matrix products, arithmetic and copies ran while one was open for 4% -> 16% of each run, Pallas kernels for 0% -> 0%
where the time goes in v1:
time: 178 us
  waiting for transfers between devices  75.2 us (42%)
  blocking collectives  35.4 us (20%)
  matrix products  16.9 us (9%)
  between operations  15.9 us (9%)
  other arithmetic  15.3 us (9%)
  local copies, waits for them, and re-layouts  13.8 us (8%)
  starting transfers between devices  5.43 us (3%)
    reduce_scatter x1, waiting for transfers between devices, body(): lax.psum_scatter(new_wv, 'island', scatter_dimension=1, tiled=True)  44.6 us
    unnamed x4, waiting for transfers between devices  30.5 us
    all_gather x1, blocking collectives, body(): rows_all = lax.all_gather(rows, 'fsdp', axis=0, tiled=True)  22.2 us
    psum x1, blocking collectives, body(): lax.psum(jnp.stack([jnp.sum(wv_grad * wv_grad), jnp.sum(own_grad * own_gr...  13.2 us
    unnamed x35, local copies, waits for them, and re-layouts  7.09 us
    convert_element_type x1, local copies, waits for them, and re-layouts, body(): standard = (cols.astype(jnp.float32) - rows_all[:, 0:1]) * rows_all[:, 1:2]  5.38 us
    all_to_all x1, starting transfers between devices, body(): lax.all_to_all(block_input, 'fsdp', split_axis=1, concat_axis=0, tiled=True)  5.3 us
    dot_general x1, matrix products, body(): jnp.dot(lang_table.astype(jnp.bfloat16).T, own_gain, preferred_element_ty...  4.57 us
  transfers between devices with their start and end apart: 4, of which 2 were waited for; matrix products, arithmetic and copies ran while one was open for 16% of the time, Pallas kernels for 0%

profile of v1, /device:TPU:0, one launch (start us, length us, event | category | flops | bytes accessed | tf_op | source)
XLA Modules:
  0.0 177.8 jit_solution(16254648224208265877)
XLA Ops:
  7.2 4.1 %copy.29 = bf16[128,8192]{0,1:T(8,128)(2,1)} copy(bf16[128,8192]{1,0:T(8,128)(2,1)} %param.11) | data formatting | bytes 4194304 | tf_op args[0]
  11.2 5.3 %all-to-all-start = ((bf16[128,8,1024]{0,2,1:T(8,128)(2,1)}), bf16[128,8,1024]{0,2,1:T(8,128)(2,1)}, u32[]{:S(2)}, u32[]{:S(2)}) async-start(bf16[128,8,1024]{0,2,1:T(8,128)(2,1)} %bitcast.1), calls=%async_computation | async-start | bytes 4194304 | tf_op jit(solution)/shard_map/all_to_all | solution.py:57
  16.7 1.2 copy.41
  17.9 0.7 copy.40
  19.1 2.2 %fusion.42 = (f32[4,8,128]{2,1,0:T(8,128)S(1)}, f32[4,8,128,128]{2,3,1,0:T(8,128)}) fusion(pred[128,128]{0,1:T(8,128)(4,1)S(1)} %iota_compare_fusion, bf16[128,4,8,128]{3,2,1,0:T(8,128)(2,1)S(1)} %bitcast.57, bf16[128,4,128,1]{2,1,0,3:T(4,128)(2,1)S(1)} %bitcast.59), kind=kOutput, calls=%fused_computation.56 | convolution fusion | flops 136315008 | bytes 3309568 | tf_op jit(solution)/shard_map/sub | solution.py:29
  21.4 2.8 %fusion.9 = bf16[4,128,128]{1,2,0:T(8,128)(2,1)} fusion(bf16[128,4,8,128]{0,3,2,1:T(8,128)(2,1)S(1)} %bitcast.56, f32[4,8,128,128]{2,3,1,0:T(8,128)} %get-tuple-element.16, f32[4,8,128]{2,1,0:T(8,128)S(1)} %get-tuple-element.15), kind=kOutput, calls=%fused_computation.20 | convolution fusion | flops 135331840 | bytes 3293184 | tf_op jit(solution)/shard_map/kgts,tkgd->skd/dot_general | solution.py:32
  24.7 0.7 fusion.2
  25.4 22.2 %all_gather.6 = f32[1024,3]{0,1:T(4,128)S(1)} all-gather(f32[128,3]{0,1:T(4,128)S(1)} %pad_maximum_fusion), channel_id=1, replica_groups=mesh['island'=4,'fsdp'=8] {'fsdp'}, dimensions={0}, use_global_device_ids=true | all-gather | bytes 13824 | tf_op jit(solution)/shard_map/all_gather | solution.py:68
  47.7 3.8 %convert_bitcast_fusion = f32[8,128,1024]{1,2,0:T(8,128)} fusion(bf16[128,8,1024]{0,2,1:T(8,128)(2,1)} %all-to-all-done), kind=kLoop, calls=%fused_computation.7 | loop fusion | flops 1048576 | bytes 6291456 | tf_op jit(solution)/shard_map/convert_element_type | solution.py:69
  51.5 5.4 %copy.30 = f32[8,128,1024]{2,1,0:T(8,128)} copy(f32[8,128,1024]{1,2,0:T(8,128)} %convert_bitcast_fusion) | data formatting | bytes 8388608 | tf_op jit(solution)/shard_map/convert_element_type | solution.py:69
  56.9 4.6 %multiply_convert_fusion = bf16[1024,1024]{1,0:T(8,128)(2,1)} fusion(f32[8,128,1024]{2,1,0:T(8,128)} %copy.30, f32[1024]{0:T(1024)S(1)} %bitcast.60, f32[1024]{0:T(1024)S(1)} %bitcast.62, f32[1024]{0:T(1024)S(1)} %bitcast.64, bf16[1,16,8192]{2,1,0:T(8,128)(2,1)} %param.17, s32[]{:T(128)S(6)} %select_n.7), kind=kOutput, calls=%fused_computation.11 | convolution fusion | flops 37765120 | bytes 6336516 | tf_op jit(solution)/shard_map/dot_general | solution.py:72
  61.5 2.4 %fusion.3 = f32[1024,1024]{1,0:T(8,128)} fusion(f32[8,128,1024]{2,1,0:T(8,128)S(1)} %copy-done, f32[1024]{0:T(1024)S(1)} %bitcast.61, f32[1024]{0:T(1024)S(1)} %bitcast.63), kind=kLoop, calls=%fused_computation.6 | loop fusion | flops 2097152 | bytes 8396800 | tf_op jit(solution)/shard_map/mul | solution.py:69
  63.8 2.7 %fusion.10 = f32[1024,1024]{1,0:T(8,128)S(1)} fusion(bf16[1024,512]{0,1:T(8,128)(2,1)} %all-gather.2.cloned.1.call-done, bf16[1,1024,512]{2,1,0:T(8,128)(2,1)S(1)} %copy-done.7), kind=kOutput, calls=%fused_computation.21 | convolution fusion | flops 1073741824 | bytes 6291456 | tf_op jit(solution)/shard_map/dot_general | solution.py:78
  66.5 2.3 %multiply_reduce_fusion.1 = (f32[]{:T(128)}, f32[16,1024]{1,0:T(8,128)S(1)}) fusion(f32[1024,1024]{1,0:T(8,128)S(1)} %copy-done.2, f32[1024,1024]{1,0:T(8,128)S(1)} %fusion.10, f32[1024]{0:T(1024)S(1)} %bitcast.65), kind=kOutput, calls=%fused_computation.33 | convolution fusion | flops 203472896 | bytes 8458244 | tf_op jit(solution)/shard_map/dot_general | solution.py:79
  68.9 2.2 %multiply_reduce_fusion = (f32[]{:T(128)}, f32[1024,512]{1,0:T(8,128)S(1)}) fusion(bf16[1024,1024]{1,0:T(8,128)(2,1)S(1)} %copy-done.3, bf16[1024,512]{0,1:T(8,128)(2,1)S(1)} %copy-done.13), kind=kOutput, calls=%fused_computation.15 | convolution fusion | flops 1075314688 | bytes 5242884 | tf_op jit(solution)/shard_map/dot_general | solution.py:77
  71.1 1.4 pad_maximum_fusion.1
  72.4 13.2 %psum.7 = f32[2]{0:T(128)S(1)} all-reduce(f32[2]{0:T(128)S(1)} %pad_maximum_fusion.1), channel_id=1, replica_groups=mesh['island'=4,'fsdp'=8] {'fsdp'}, use_global_device_ids=true, to_apply=%region_6.7 | all-reduce | flops 2 | bytes 16 | tf_op jit(solution)/shard_map/psum | solution.py:82
  87.6 1.4 multiply_subtract_fusion.3
  89.0 1.7 multiply_subtract_fusion
  90.8 0.6 copy-done.15
  92.6 30.5 %all-reduce.3.cloned.1.call-done = f32[16,1024]{1,0:T(8,128)} async-done(((f32[16,1024]{1,0:T(8,128)}), f32[16,1024]{1,0:T(8,128)}) %all-reduce.3.cloned.1.call-update) | async-done | bytes 65552
  123.1 1.4 multiply_subtract_fusion.4
  124.5 44.6 %reduce-scatter.2.cloned.1.call-done = f32[1024,128]{1,0:T(8,128)} async-done(((f32[1024,512]{1,0:T(8,128)}), f32[1024,128]{1,0:T(8,128)}) %reduce-scatter.2.cloned.1.call-update) | async-done | bytes 524304 | tf_op jit(solution)/shard_map/reduce_scatter | solution.py:87
  169.1 2.1 %multiply_subtract_fusion.1 = (f32[1024,128]{1,0:T(8,128)}, f32[1024,128]{1,0:T(8,128)}) fusion(f32[1024,128]{1,0:T(8,128)S(1)} %copy-done.8, f32[1024,128]{1,0:T(8,128)} %reduce-scatter.2.cloned.1.call-done, f32[1024,128]{1,0:T(8,128)S(1)} %copy-done.9), kind=kLoop, calls=%fused_computation.28 | loop fusion | flops 1048576 | bytes 2621440 | tf_op jit(solution)/shard_map/sub | solution.py:91
  (49 shorter events, 2.4 us)
Async XLA Ops:
  11.2 5.4 %copy-start.10 = (bf16[128,512]{1,0:T(8,128)(2,1)S(1)}, bf16[128,512]{1,0:T(8,128)(2,1)}, u32[]{:S(2)}) copy-start(bf16[128,512]{1,0:T(8,128)(2,1)} %param.14) | copy-start | bytes 393220
  11.2 5.4 %copy-start.4 = (bf16[128,4096]{1,0:T(8,128)(2,1)S(1)}, bf16[128,4096]{1,0:T(8,128)(2,1)}, u32[]{:S(2)}) copy-start(bf16[128,4096]{1,0:T(8,128)(2,1)} %param.13) | copy-start | bytes 3145732
  11.2 36.4 %all-to-all-start = ((bf16[128,8,1024]{0,2,1:T(8,128)(2,1)}), bf16[128,8,1024]{0,2,1:T(8,128)(2,1)}, u32[]{:S(2)}, u32[]{:S(2)}) async-start(bf16[128,8,1024]{0,2,1:T(8,128)(2,1)} %bitcast.1), calls=%async_computation | async-start | bytes 4194304 | tf_op jit(solution)/shard_map/all_to_all | solution.py:57
  16.6 1.3 copy-start.5
  16.6 47.3 %all-gather.2.cloned.1.call-start = ((), (), s32[]{:S(2)}) async-start(), calls=%async_computation.2 | async-start | bytes 1179648 | tf_op jit(solution)/shard_map/all_gather | solution.py:58
  17.9 1.2 copy-start.6
  21.4 2.9 %copy-start.1 = (bf16[128,8192]{1,0:T(8,128)(2,1)S(1)}, bf16[128,8192]{1,0:T(8,128)(2,1)}, u32[]{:S(2)}) copy-start(bf16[128,8192]{1,0:T(8,128)(2,1)} %param.11) | copy-start | bytes 6291460
  24.2 1.2 copy-start.14
  24.2 98.9 %all-reduce.3.cloned.1.call-start = ((), (), s32[]{:S(2)}) async-start(), calls=%async_computation.4 | async-start | bytes 131072
  56.9 4.6 %copy-start = (f32[8,128,1024]{2,1,0:T(8,128)S(1)}, f32[8,128,1024]{2,1,0:T(8,128)}, u32[]{:S(2)}) copy-start(f32[8,128,1024]{2,1,0:T(8,128)} %copy.30) | copy-start | bytes 12582916
  61.5 2.4 %copy-start.7 = (bf16[1,1024,512]{2,1,0:T(8,128)(2,1)S(1)}, bf16[1,1024,512]{2,1,0:T(8,128)(2,1)}, u32[]{:S(2)}) copy-start(bf16[1,1024,512]{2,1,0:T(8,128)(2,1)} %param.16) | copy-start | bytes 3145732
  63.8 2.7 %copy-start.2 = (f32[1024,1024]{1,0:T(8,128)S(1)}, f32[1024,1024]{1,0:T(8,128)}, u32[]{:S(2)}) copy-start(f32[1024,1024]{1,0:T(8,128)} %fusion.3) | copy-start | bytes 12582916
  66.5 2.4 %copy-start.3 = (bf16[1024,1024]{1,0:T(8,128)(2,1)S(1)}, bf16[1024,1024]{1,0:T(8,128)(2,1)}, u32[]{:S(2)}) copy-start(bf16[1024,1024]{1,0:T(8,128)(2,1)} %multiply_convert_fusion) | copy-start | bytes 6291460
  66.5 2.3 %copy-start.13 = (bf16[1024,512]{0,1:T(8,128)(2,1)S(1)}, bf16[1024,512]{0,1:T(8,128)(2,1)}, u32[]{:S(2)}) copy-start(bf16[1024,512]{0,1:T(8,128)(2,1)} %all-gather.2.cloned.1.call-done) | copy-start | bytes 3145732
  89.0 80.1 %reduce-scatter.2.cloned.1.call-start = ((), (), s32[]{:S(2)}) async-start(), calls=%async_computation.3 | async-start | bytes 2621440 | tf_op jit(solution)/shard_map/reduce_scatter | solution.py:87
  90.7 0.7 copy-start.15
  90.7 32.4 %copy-start.11 = (f32[4,1024]{1,0:T(4,128)S(1)}, f32[4,1024]{1,0:T(4,128)}, u32[]{:S(2)}) copy-start(f32[4,1024]{1,0:T(4,128)} %param.20) | copy-start | bytes 49156
  90.7 32.4 %copy-start.12 = (f32[4,1024]{1,0:T(4,128)S(1)}, f32[4,1024]{1,0:T(4,128)}, u32[]{:S(2)}) copy-start(f32[4,1024]{1,0:T(4,128)} %param.21) | copy-start | bytes 49156
  90.7 78.4 %copy-start.8 = (f32[1024,128]{1,0:T(8,128)S(1)}, f32[1024,128]{1,0:T(8,128)}, u32[]{:S(2)}) copy-start(f32[1024,128]{1,0:T(8,128)} %param.18) | copy-start | bytes 1572868
  90.7 78.4 %copy-start.9 = (f32[1024,128]{1,0:T(8,128)S(1)}, f32[1024,128]{1,0:T(8,128)}, u32[]{:S(2)}) copy-start(f32[1024,128]{1,0:T(8,128)} %param.19) | copy-start | bytes 1572868
Sparse Core Ops, SparseCore 0:
  24.4 28.1 all-gather.1
  89.1 33.9 all-reduce.2
  125.5 43.5 reduce-scatter.1

commit v2 on v1

v2 whole, which is shorter than its diff:
```python
import functools

import jax
import jax.numpy as jnp
from jax import lax
from jax.experimental import pallas as pl
from jax.experimental.pallas import tpu as pltpu
from jax.sharding import PartitionSpec as P

HEADS = 32
KV_HEADS = 4
HEAD_DIM = 128


EPSILON = 1e-05
MOMENTUM = 0.9
OUTER_RATE = 0.7
CLIP_SHARE = 0.25


def value_grad(query_rows, key_block, grad_rows):
    length = query_rows.shape[0]
    group = HEADS // KV_HEADS
    query_four = query_rows.reshape(length, KV_HEADS, group, HEAD_DIM)
    key_three = key_block.reshape(length, KV_HEADS, HEAD_DIM)
    scores = jnp.einsum(
        "tkgd,skd->kgts", query_four, key_three, preferred_element_type=jnp.float32
    ) * HEAD_DIM ** (-0.5)
    position = jnp.arange(length, dtype=jnp.int32)
    causal = position[:, None] >= position[None, :]
    scores = jnp.where(causal, scores, -jnp.inf)
    row_top = jnp.max(scores, axis=-1, keepdims=True)
    exponent = jnp.exp(scores - row_top)
    weights_bf = (exponent / jnp.sum(exponent, axis=-1, keepdims=True)).astype(jnp.bfloat16)
    grad_four = grad_rows.reshape(length, KV_HEADS, group, HEAD_DIM)
    values = jnp.einsum("kgts,tkgd->skd", weights_bf, grad_four, preferred_element_type=jnp.float32)
    return values.reshape(length, KV_HEADS * HEAD_DIM).astype(jnp.bfloat16)


def totals_by_collectives(
    block_input,
    lang_ids,
    queries,
    saved_keys,
    out_grad,
    local_wv,
    local_gain,
):
    width = block_input.shape[1]
    fsdp_count = lax.axis_size("fsdp")
    col_block = width // fsdp_count
    kv_width = local_wv.shape[2]
    lang_count = local_gain.shape[1]
    weight_scale = width ** (-0.5)
    col_begin = lax.axis_index("fsdp") * col_block
    cols = lax.all_to_all(block_input, "fsdp", split_axis=1, concat_axis=0, tiled=True)
    values_all = lax.all_gather(
        value_grad(queries, saved_keys, out_grad), "fsdp", axis=0, tiled=True
    )
    widened = block_input.astype(jnp.float32)
    average = jnp.mean(widened, axis=-1, keepdims=True)
    centered = widened - average
    variance = jnp.mean(centered * centered, axis=-1, keepdims=True)
    rows = jnp.concatenate(
        [average, lax.rsqrt(variance + EPSILON), lang_ids[:, None].astype(jnp.float32)], axis=1
    )
    rows_all = lax.all_gather(rows, "fsdp", axis=0, tiled=True)
    standard = (cols.astype(jnp.float32) - rows_all[:, 0:1]) * rows_all[:, 1:2]
    lang_table = rows_all[:, 2][None, :] == jnp.arange(lang_count, dtype=jnp.float32)[:, None]
    own_gain = lax.dynamic_slice_in_dim(local_gain[0], col_begin, col_block, 1)
    gain_rows = jnp.dot(
        lang_table.astype(jnp.bfloat16).T, own_gain, preferred_element_type=jnp.float32
    )
    normed = (standard * gain_rows).astype(jnp.bfloat16)
    weight_rows = local_wv[0]
    wv_grad = jnp.dot(normed.T, values_all, preferred_element_type=jnp.float32) * weight_scale
    input_grad = jnp.dot(values_all, weight_rows.T, preferred_element_type=jnp.float32) * weight_scale
    own_grad = jnp.dot(
        lang_table.astype(jnp.float32), standard * input_grad, precision=lax.Precision.HIGHEST
    )
    squares = lax.psum(jnp.stack([jnp.sum(wv_grad * wv_grad), jnp.sum(own_grad * own_grad)]), "fsdp")
    wv_clip = jnp.minimum(1.0, CLIP_SHARE * (width * kv_width) ** 0.5 / jnp.sqrt(squares[0]))
    gain_clip = jnp.minimum(1.0, CLIP_SHARE * (lang_count * width) ** 0.5 / jnp.sqrt(squares[1]))
    new_wv = weight_rows.astype(jnp.float32) - wv_clip * wv_grad
    new_gain = own_gain.astype(jnp.float32) - gain_clip * own_grad
    total_wv = lax.psum_scatter(new_wv, "island", scatter_dimension=1, tiled=True)
    total_gain = lax.psum_scatter(new_gain, "island", scatter_dimension=0, tiled=True)
    return total_wv, total_gain


CHUNKS = 4
EARLY = 2


def remote(src, dst, send_sem, recv_sem, where):
    return pltpu.make_async_remote_copy(
        src_ref=src,
        dst_ref=dst,
        send_sem=send_sem,
        recv_sem=recv_sem,
        device_id=where,
        device_id_type=pl.DeviceIdType.MESH,
    )


def attend(q_v, k_v, og_v):
    length = q_v.shape[0]
    group = HEADS // KV_HEADS
    at = lax.broadcasted_iota(jnp.int32, (length, length), 0)
    key_at = lax.broadcasted_iota(jnp.int32, (length, length), 1)
    bias = jnp.where(at >= key_at, 0.0, -1e30).astype(jnp.float32)
    bias = jnp.concatenate([bias] * group, axis=0)
    parts = []
    for j in range(KV_HEADS):
        heads = [slice((j * group + g) * HEAD_DIM, (j * group + g + 1) * HEAD_DIM) for g in range(group)]
        q = jnp.concatenate([q_v[:, h] for h in heads], axis=0)
        k = k_v[:, j * HEAD_DIM : (j + 1) * HEAD_DIM]
        scores = lax.dot_general(q, k, (((1,), (1,)), ((), ())), preferred_element_type=jnp.float32)
        scores = scores * HEAD_DIM ** (-0.5) + bias
        exponent = jnp.exp(scores - jnp.max(scores, axis=1, keepdims=True))
        probs = (exponent / jnp.sum(exponent, axis=1, keepdims=True)).astype(jnp.bfloat16)
        og = jnp.concatenate([og_v[:, h] for h in heads], axis=0)
        parts.append(
            lax.dot_general(probs, og, (((0,), (0,)), ((), ())), preferred_element_type=jnp.float32)
        )
    return jnp.concatenate(parts, axis=1).astype(jnp.bfloat16)


def kernel(
    nf, ni,
    x_hbm, lang_ref, q_hbm, k_hbm, og_hbm, wv_hbm, gain_ref,
    tot_wv, tot_gain,
    x_v, q_v, k_v, og_v, wv_v, x_buf, v_buf, s_buf, mean_b, rstd_b, hot, normed,
    g_own, g_send, g_buf, lw_buf, gg_send, gg_buf, sq_buf, clip_buf,
    load_sem, own_sem, x_ss, x_rs, lw_ss, lw_rs, v_ss, v_rs, fw_ss, s_ss, s_rs,
    g_ss, g_rs, gg_ss, gg_rs, sq_ss, sq_rs, c_ss, c_rs,
):
    f = lax.axis_index("fsdp")
    i = lax.axis_index("island")
    tokens, width = x_v.shape
    kv_width = wv_v.shape[1]
    langs = gain_ref.shape[0]
    cols = width // nf
    chunk = cols // CHUNKS
    share = kv_width // ni
    gain_share = langs // ni
    scale = width ** (-0.5)
    peers = [lax.rem(f + d, nf) for d in range(1, nf)]
    zpeers = [lax.rem(i + d, ni) for d in range(1, ni)]
    core = lax.rem(f, 2)
    chip = f // 2
    sibling = chip * 2 + 1 - core
    mates = [lax.rem(chip + d, nf // 2) * 2 + core for d in range(1, nf // 2)]
    others = [lax.rem(chip + d, nf // 2) * 2 + 1 - core for d in range(1, nf // 2)]

    loads = [
        pltpu.make_async_copy(src, dst, load_sem.at[n])
        for n, (src, dst) in enumerate(
            [(q_hbm, q_v), (k_hbm, k_v), (og_hbm, og_v), (x_hbm, x_v), (wv_hbm, wv_v)]
        )
    ]
    for copy in loads:
        copy.start()

    def x_cols(owner, k):
        return pl.ds(pl.multiple_of(owner * cols + k * chunk, 128), chunk)

    own_copies = [
        pltpu.make_async_copy(x_hbm.at[:, x_cols(f, k)], x_buf.at[k, f], own_sem.at[k])
        for k in range(CHUNKS)
    ]
    for copy in own_copies:
        copy.start()

    barrier = pltpu.get_barrier_semaphore()
    for p in peers:
        pl.semaphore_signal(barrier, inc=1, device_id={"fsdp": p}, device_id_type=pl.DeviceIdType.MESH)
    for p in zpeers:
        pl.semaphore_signal(barrier, inc=1, device_id={"island": p}, device_id_type=pl.DeviceIdType.MESH)
    pl.semaphore_wait(barrier, nf - 1 + ni - 1)

    def x_copy(k, p):
        return remote(x_hbm.at[:, x_cols(p, k)], x_buf.at[k, f], x_ss.at[k, p], x_rs.at[k, f], {"fsdp": p})

    def x_wait(k, p):
        remote(x_hbm.at[:, x_cols(p, k)], x_buf.at[k, p], x_ss.at[k, p], x_rs.at[k, p], {"fsdp": p}).wait_recv()

    for k in range(EARLY):
        for p in peers:
            x_copy(k, p).start()

    def lw_copy(p, slot):
        src = wv_hbm.at[:, pl.ds(pl.multiple_of(p * share, 128), share)]
        return remote(src, lw_buf.at[slot], lw_ss.at[p], lw_rs.at[slot], {"island": p})

    for p in zpeers:
        lw_copy(p, i).start()

    for copy in loads[:3]:
        copy.wait()
    v_buf[f] = attend(q_v, k_v, og_v)

    def v_copy(slot, p, send_sem):
        return remote(v_buf.at[slot], v_buf.at[slot], send_sem, v_rs.at[slot], {"fsdp": p})

    for p in mates:
        v_copy(f, p, v_ss.at[p]).start()
    v_copy(f, sibling, v_ss.at[sibling]).start()
    for k in range(EARLY, CHUNKS):
        for p in peers:
            x_copy(k, p).start()

    loads[3].wait()
    widened = x_v[...].astype(jnp.float32)
    average = jnp.mean(widened, axis=1, keepdims=True)
    centered = x_v[...].astype(jnp.float32) - average
    rstd = lax.rsqrt(jnp.mean(centered * centered, axis=1, keepdims=True) + EPSILON)
    square = (tokens, tokens)
    eye = lax.broadcasted_iota(jnp.int32, square, 0) == lax.broadcasted_iota(jnp.int32, square, 1)

    def to_row(column):
        return jnp.sum(jnp.where(eye, jnp.broadcast_to(column, square), 0.0), axis=0, keepdims=True)

    def to_column(row):
        return jnp.sum(jnp.where(eye, jnp.broadcast_to(row, square), 0.0), axis=1, keepdims=True)

    s_buf[f] = jnp.concatenate(
        [to_row(average), to_row(rstd), lang_ref[...].astype(jnp.float32), jnp.zeros((5, tokens), jnp.float32)],
        axis=0,
    )

    def s_copy(slot, p):
        return remote(s_buf.at[slot], s_buf.at[slot], s_ss.at[p], s_rs.at[slot], {"fsdp": p})

    for p in peers:
        s_copy(f, p).start()
    for p in mates:
        v_copy(p, p, v_ss.at[p]).wait_recv()
        v_copy(p, sibling, fw_ss.at[p]).start()

    loads[4].wait()
    for copy in own_copies:
        copy.wait()
    for p in peers:
        s_copy(p, p).wait_recv()
    for s in range(nf):
        stats = s_buf[s]
        rows = pl.ds(s * tokens, tokens)
        mean_b[rows, :] = jnp.broadcast_to(to_column(stats[0:1]), square)
        rstd_b[rows, :] = jnp.broadcast_to(to_column(stats[1:2]), square)
        kinds = lax.broadcasted_iota(jnp.int32, (langs, tokens), 0).astype(jnp.float32)
        hot[:, s * tokens : (s + 1) * tokens] = jnp.where(
            jnp.broadcast_to(stats[2:3], (langs, tokens)) == kinds, 1.0, 0.0
        ).astype(jnp.bfloat16)
    v_copy(sibling, sibling, v_ss.at[sibling]).wait_recv()
    for p in others:
        v_copy(p, sibling, v_ss.at[p]).wait_recv()

    def g_copy(k, p, slot):
        rows = pl.ds(pl.multiple_of(k * chunk, 128), chunk)
        return remote(g_send.at[p, rows], g_buf.at[slot, rows], g_ss.at[k, p], g_rs.at[k, slot], {"island": p})

    def step(k, carry):
        wv_square, gain_square = carry
        for p in peers:
            x_wait(k, p)
        rows = pl.ds(pl.multiple_of(k * chunk, 128), chunk)
        weight = wv_v[rows, :]
        gain = gain_ref[:, pl.ds(pl.multiple_of(f * cols + k * chunk, 128), chunk)]
        gain_grad = jnp.zeros((langs, chunk), jnp.float32)
        for s in range(nf):
            at = slice(s * tokens, (s + 1) * tokens)
            mean = jnp.concatenate([mean_b[at, :]] * (chunk // tokens), axis=1)
            rstd = jnp.concatenate([rstd_b[at, :]] * (chunk // tokens), axis=1)
            table = hot[:, at]
            standard = (x_buf[k, s].astype(jnp.float32) - mean) * rstd
            gain_rows = lax.dot_general(table, gain, (((0,), (0,)), ((), ())), preferred_element_type=jnp.float32)
            normed[at, :] = (standard * gain_rows).astype(jnp.bfloat16)
            input_grad = (
                lax.dot_general(v_buf[s], weight, (((1,), (1,)), ((), ())), preferred_element_type=jnp.float32) * scale
            )
            product = standard * input_grad
            high = product.astype(jnp.bfloat16)
            rest = product - high.astype(jnp.float32)
            middle = rest.astype(jnp.bfloat16)
            low = (rest - middle.astype(jnp.float32)).astype(jnp.bfloat16)
            for piece in (high, middle, low):
                gain_grad = gain_grad + jnp.dot(table, piece, preferred_element_type=jnp.float32)
        values_all = v_buf[...].reshape(nf * tokens, kv_width)
        grad = (
            lax.dot_general(normed[...], values_all, (((0,), (0,)), ((), ())), preferred_element_type=jnp.float32)
            * scale
        )
        for j in range(ni):
            piece = grad[:, j * share : (j + 1) * share]
            g_own[j, rows, :] = piece
            g_send[j, rows, :] = piece.astype(jnp.bfloat16)
            own = slice(j * gain_share, (j + 1) * gain_share)
            gg_send[j, 0:gain_share, rows] = gain[own].astype(jnp.float32)
            gg_send[j, gain_share : 2 * gain_share, rows] = gain_grad[own]
        for p in zpeers:
            g_copy(k, p, i).start()
        return (
            wv_square + jnp.sum(grad * grad, axis=0, keepdims=True),
            gain_square + jnp.sum(gain_grad * gain_grad, axis=0, keepdims=True),
        )

    start = (jnp.zeros((1, kv_width), jnp.float32), jnp.zeros((1, chunk), jnp.float32))
    wv_square, gain_square = lax.fori_loop(0, CHUNKS, step, start)

    tile = (8, 128)
    first = lax.broadcasted_iota(jnp.int32, tile, 0) == 0
    sq_buf[f] = jnp.where(
        first,
        jnp.broadcast_to(jnp.sum(wv_square, axis=1, keepdims=True), tile),
        jnp.broadcast_to(jnp.sum(gain_square, axis=1, keepdims=True), tile),
    )

    def sq_copy(slot, p):
        return remote(sq_buf.at[slot], sq_buf.at[slot], sq_ss.at[p], sq_rs.at[slot], {"fsdp": p})

    def gg_copy(p, slot):
        return remote(gg_send.at[p], gg_buf.at[slot], gg_ss.at[p], gg_rs.at[slot], {"island": p})

    for p in peers:
        sq_copy(f, p).start()
    for p in zpeers:
        gg_copy(p, i).start()
    for p in peers:
        sq_copy(p, p).wait_recv()
    norm = jnp.sqrt(jnp.sum(sq_buf[...], axis=0))
    bound = jnp.where(first, CLIP_SHARE * (width * kv_width) ** 0.5, CLIP_SHARE * (langs * width) ** 0.5)
    clip_buf[i] = jnp.minimum(1.0, bound.astype(jnp.float32) / norm)

    def c_copy(slot, p):
        return remote(clip_buf.at[slot], clip_buf.at[slot], c_ss.at[p], c_rs.at[slot], {"island": p})

    for p in zpeers:
        c_copy(i, p).start()
    for p in zpeers:
        lw_copy(p, p).wait_recv()
        gg_copy(p, p).wait_recv()
        c_copy(p, p).wait_recv()
    for k in range(CHUNKS):
        for p in zpeers:
            g_copy(k, p, p).wait_recv()

    def wide(row, size):
        return jnp.concatenate([row] * (size // 128), axis=1)

    mine = clip_buf[i]
    own_gain = gg_send[i]
    total = own_gain[0:gain_share] - wide(mine[1:2], cols) * own_gain[gain_share : 2 * gain_share]
    for p in zpeers:
        theirs = gg_buf[p]
        total = total + theirs[0:gain_share] - wide(clip_buf[p][1:2], cols) * theirs[gain_share : 2 * gain_share]
    tot_gain[...] = total
    total = wv_v[:, pl.ds(pl.multiple_of(i * share, 128), share)].astype(jnp.float32) - mine[0:1] * g_own[i]
    for p in zpeers:
        total = total + lw_buf[p].astype(jnp.float32) - clip_buf[p][0:1] * g_buf[p].astype(jnp.float32)
    tot_wv[...] = total

    for p in peers:
        for k in range(CHUNKS):
            x_copy(k, p).wait_send()
        s_copy(f, p).wait_send()
        sq_copy(f, p).wait_send()
    for p in mates:
        v_copy(f, p, v_ss.at[p]).wait_send()
        v_copy(p, sibling, fw_ss.at[p]).wait_send()
    v_copy(f, sibling, v_ss.at[sibling]).wait_send()
    for p in zpeers:
        lw_copy(p, i).wait_send()
        gg_copy(p, i).wait_send()
        c_copy(i, p).wait_send()
        for k in range(CHUNKS):
            g_copy(k, p, i).wait_send()


def totals_by_kernel(block_input, lang_ids, queries, saved_keys, out_grad, local_wv, local_gain):
    nf, ni = lax.axis_size("fsdp"), lax.axis_size("island")
    tokens, width = block_input.shape
    kv_width, langs = local_wv.shape[2], local_gain.shape[1]
    cols = width // nf
    chunk, share, gain_share = cols // CHUNKS, kv_width // ni, langs // ni
    bf, f32 = jnp.bfloat16, jnp.float32
    vmem = lambda *shape, dtype=bf: pltpu.VMEM(shape, dtype)
    dma = pltpu.SemaphoreType.DMA
    hbm = pl.BlockSpec(memory_space=pl.ANY)
    held = pl.BlockSpec(memory_space=pltpu.VMEM)
    return pl.pallas_call(
        functools.partial(kernel, nf, ni),
        out_shape=(jax.ShapeDtypeStruct((cols, share), f32), jax.ShapeDtypeStruct((gain_share, cols), f32)),
        in_specs=[hbm, held, hbm, hbm, hbm, hbm, held],
        out_specs=(held, held),
        scratch_shapes=[
            vmem(tokens, width),
            vmem(*queries.shape),
            vmem(*saved_keys.shape),
            vmem(*out_grad.shape),
            vmem(cols, kv_width),
            vmem(CHUNKS, nf, tokens, chunk),
            vmem(nf, tokens, kv_width),
            vmem(nf, 8, tokens, dtype=f32),
            vmem(nf * tokens, tokens, dtype=f32),
            vmem(nf * tokens, tokens, dtype=f32),
            vmem(langs, nf * tokens),
            vmem(nf * tokens, chunk),
            vmem(ni, cols, share, dtype=f32),
            vmem(ni, cols, share),
            vmem(ni, cols, share),
            vmem(ni, cols, share),
            vmem(ni, 2 * gain_share, cols, dtype=f32),
            vmem(ni, 2 * gain_share, cols, dtype=f32),
            vmem(nf, 8, 128, dtype=f32),
            vmem(ni, 8, 128, dtype=f32),
            dma((5,)),
            dma((CHUNKS,)),
            dma((CHUNKS, nf)),
            dma((CHUNKS, nf)),
            dma((ni,)),
            dma((ni,)),
            dma((nf,)),
            dma((nf,)),
            dma((nf,)),
            dma((nf,)),
            dma((nf,)),
            dma((CHUNKS, ni)),
            dma((CHUNKS, ni)),
            dma((ni,)),
            dma((ni,)),
            dma((nf,)),
            dma((nf,)),
            dma((ni,)),
            dma((ni,)),
        ],
        compiler_params=pltpu.CompilerParams(
            collective_id=0, has_side_effects=True, vmem_limit_bytes=48 * 1024 * 1024
        ),
    )(block_input, lang_ids[None, :], queries, saved_keys, out_grad, local_wv[0], local_gain[0])


def body(
    block_input,
    lang_ids,
    queries,
    saved_keys,
    out_grad,
    local_wv,
    local_gain,
    outer_wv,
    wv_momentum,
    outer_gain,
    gain_momentum,
):
    island_count = lax.axis_size("island")
    fsdp_count = lax.axis_size("fsdp")
    whole_tiles = (
        local_wv.shape[2] % (128 * island_count) == 0
        and local_gain.shape[1] % (4 * island_count) == 0
        and block_input.shape[1] % (128 * CHUNKS * fsdp_count) == 0
        and block_input.shape[0] == 128
        and fsdp_count % 2 == 0
    )
    totals = totals_by_kernel if whole_tiles else totals_by_collectives
    total_wv, total_gain = totals(
        block_input, lang_ids, queries, saved_keys, out_grad, local_wv, local_gain
    )
    delta_wv = outer_wv - total_wv / island_count
    momentum_wv = MOMENTUM * wv_momentum + delta_wv
    result_wv = outer_wv - OUTER_RATE * (delta_wv + MOMENTUM * momentum_wv)
    delta_gain = outer_gain - total_gain / island_count
    momentum_gain = MOMENTUM * gain_momentum + delta_gain
    result_gain = outer_gain - OUTER_RATE * (delta_gain + MOMENTUM * momentum_gain)
    return (result_wv, momentum_wv, result_gain, momentum_gain)


def solution(mesh):
    in_specs = (
        P(("island", "fsdp"), None),
        P(("island", "fsdp")),
        P(("island", "fsdp"), None),
        P(("island", "fsdp"), None),
        P(("island", "fsdp"), None),
        P("island", "fsdp", None),
        P("island", None, None),
        P("fsdp", "island"),
        P("fsdp", "island"),
        P("island", "fsdp"),
        P("island", "fsdp"),
    )
    out_specs = (P("fsdp", "island"), P("fsdp", "island"), P("island", "fsdp"), P("island", "fsdp"))
    return jax.shard_map(body, mesh=mesh, in_specs=in_specs, out_specs=out_specs, check_vma=False)
```

time: 178 us -> 79 us (0.44)
  waiting for transfers between devices: 75.2 us -> 0 us
  Pallas kernels: 0 us -> 68.5 us
  blocking collectives: 35.4 us -> 0 us
  matrix products: 16.9 us -> 0 us
  between operations: 15.9 us -> 0.69 us
  other arithmetic: 15.3 us -> 1.73 us
  local copies, waits for them, and re-layouts: 13.8 us -> 7.78 us
  starting transfers between devices: 5.43 us -> 0 us
    pallas_call x0 -> x1, Pallas kernels: none -> 68.5 us  [totals_by_kernel(): pl.pallas_call(functools.partial(kernel, nf, ni), out_shape=(jax.ShapeDty...]
    reduce_scatter x1 -> x0, waiting for transfers between devices: 44.6 us -> none  [body(): lax.psum_scatter(new_wv, 'island', scatter_dimension=1, tiled=True)]
    unnamed x4 -> x0, waiting for transfers between devices: 30.5 us -> none
    all_gather x1 -> x0, blocking collectives: 22.2 us -> none  [body(): rows_all = lax.all_gather(rows, 'fsdp', axis=0, tiled=True)]
    dot_general x5 -> x0, matrix products: 14.6 us -> none  [the longest x1 4.57 us: body(): jnp.dot(lang_table.astype(jnp.bfloat16).T, own_gain, preferred_element_ty...]
    psum x1 -> x0, blocking collectives: 13.2 us -> none  [body(): lax.psum(jnp.stack([jnp.sum(wv_grad * wv_grad), jnp.sum(own_grad * own_gr...]
    convert_element_type x1 -> x0, local copies, waits for them, and re-layouts: 5.38 us -> none  [body(): standard = (cols.astype(jnp.float32) - rows_all[:, 0:1]) * rows_all[:, 1:2]]
    all_to_all x1 -> x0, starting transfers between devices: 5.3 us -> none  [body(): lax.all_to_all(block_input, 'fsdp', split_axis=1, concat_axis=0, tiled=True)]
  transfers between devices with their start and end apart: 4 -> 0, of which waited for: 2 -> 0; matrix products, arithmetic and copies ran while one was open for 16% -> 0% of each run, Pallas kernels for 0% -> 0%
where the time goes in v2:
time: 79 us; the launch traced here: 78.7 us
  Pallas kernels  68.5 us (87%)
  local copies, waits for them, and re-layouts  7.78 us (10%)
  other arithmetic  1.73 us (2%)
    pallas_call x1, Pallas kernels, totals_by_kernel(): pl.pallas_call(functools.partial(kernel, nf, ni), out_shape=(jax.ShapeDty...  68.5 us
    unnamed x22, local copies, waits for them, and re-layouts  7.78 us

profile of v2, /device:TPU:0, one launch (start us, length us, event | category | flops | bytes accessed | tf_op | source)
XLA Modules:
  0.0 78.7 jit_solution(4041797356961624448)
XLA Ops:
  0.6 0.0 copy-start
  0.6 1.6 %copy-done = bf16[128,8192]{1,0:T(8,128)(2,1)S(1)} copy-done((bf16[128,8192]{1,0:T(8,128)(2,1)S(1)}, bf16[128,8192]{1,0:T(8,128)(2,1)}, u32[]{:S(2)}) %copy-start) | copy-done | bytes 2097176
  2.2 1.2 %copy-done.1 = bf16[128,4096]{1,0:T(8,128)(2,1)S(1)} copy-done((bf16[128,4096]{1,0:T(8,128)(2,1)S(1)}, bf16[128,4096]{1,0:T(8,128)(2,1)}, u32[]{:S(2)}) %copy-start.1) | copy-done | bytes 1048600
  3.5 0.0 copy-start.2
  3.5 1.2 %copy-done.2 = bf16[128,4096]{1,0:T(8,128)(2,1)S(1)} copy-done((bf16[128,4096]{1,0:T(8,128)(2,1)S(1)}, bf16[128,4096]{1,0:T(8,128)(2,1)}, u32[]{:S(2)}) %copy-start.2) | copy-done | bytes 1048600
  4.7 0.0 copy-start.3
  4.7 1.2 %copy-done.3 = bf16[1,1024,512]{2,1,0:T(8,128)(2,1)S(1)} copy-done((bf16[1,1024,512]{2,1,0:T(8,128)(2,1)S(1)}, bf16[1,1024,512]{2,1,0:T(8,128)(2,1)}, u32[]{:S(2)}) %copy-start.3) | copy-done | bytes 1048600
  5.9 0.0 copy-start.4
  5.9 0.9 %copy-done.4 = bf16[1,16,8192]{2,1,0:T(8,128)(2,1)S(1)} copy-done((bf16[1,16,8192]{2,1,0:T(8,128)(2,1)S(1)}, bf16[1,16,8192]{2,1,0:T(8,128)(2,1)}, u32[]{:S(2)}) %copy-start.4) | copy-done | bytes 262168
  6.9 0.0 copy-start.5
  6.9 0.9 %copy-done.5 = bf16[128,512]{1,0:T(8,128)(2,1)S(1)} copy-done((bf16[128,512]{1,0:T(8,128)(2,1)S(1)}, bf16[128,512]{1,0:T(8,128)(2,1)}, u32[]{:S(2)}) %copy-start.5) | copy-done | bytes 131096
  7.8 0.0 copy-start.6
  7.8 0.7 copy-done.6
  8.4 0.0 copy-start.7
  8.4 0.0 copy-start.8
  8.4 68.5 %shard_map.138 = (f32[1024,128]{1,0:T(8,128)S(1)}, f32[4,1024]{1,0:T(4,128)S(1)}) custom-call(bf16[128,8192]{1,0:T(8,128)(2,1)S(1)} %copy-done, s32[1,128]{1,0:T(1,128)S(1)} %bitcast.5, bf16[128,4096]{1,0:T(8,128)(2,1)S(1)} %copy-done.1, bf16[128,512]{1,0:T(8,128)(2,1)S(1)} %copy-done.5, bf16[128,4096]{1,0:T(8,128)(2,1)S(1)} %copy-done.2, ...), custom_call_target="tpu_custom_call" | custom-call | tf_op jit(solution)/shard_map/pallas_call | solution.py:391
  76.9 0.0 copy-start.9
  76.9 0.0 copy-start.10
  76.9 0.0 copy-done.7
  76.9 0.0 copy-done.8
  76.9 1.1 %multiply_subtract_fusion = (f32[1024,128]{1,0:T(8,128)}, f32[1024,128]{1,0:T(8,128)}) fusion(f32[1024,128]{1,0:T(8,128)S(1)} %copy-done.7, f32[1024,128]{1,0:T(8,128)S(1)} %get-tuple-element.6, f32[1024,128]{1,0:T(8,128)S(1)} %copy-done.8), kind=kLoop, calls=%fused_computation | loop fusion | flops 1048576 | bytes 2621440 | tf_op jit(solution)/shard_map/sub | solution.py:471
  78.0 0.0 copy-done.9
  78.0 0.0 copy-done.10
  78.0 0.6 multiply_subtract_fusion.2
  (1 shorter events, 0.0 us)
Async XLA Ops:
  0.6 1.6 %copy-start = (bf16[128,8192]{1,0:T(8,128)(2,1)S(1)}, bf16[128,8192]{1,0:T(8,128)(2,1)}, u32[]{:S(2)}) copy-start(bf16[128,8192]{1,0:T(8,128)(2,1)} %x_hbm.1) | copy-start | bytes 6291460
  2.2 1.2 %copy-start.1 = (bf16[128,4096]{1,0:T(8,128)(2,1)S(1)}, bf16[128,4096]{1,0:T(8,128)(2,1)}, u32[]{:S(2)}) copy-start(bf16[128,4096]{1,0:T(8,128)(2,1)} %q_hbm.1) | copy-start | bytes 3145732
  3.5 1.2 %copy-start.2 = (bf16[128,4096]{1,0:T(8,128)(2,1)S(1)}, bf16[128,4096]{1,0:T(8,128)(2,1)}, u32[]{:S(2)}) copy-start(bf16[128,4096]{1,0:T(8,128)(2,1)} %og_hbm.1) | copy-start | bytes 3145732
  4.7 1.2 %copy-start.3 = (bf16[1,1024,512]{2,1,0:T(8,128)(2,1)S(1)}, bf16[1,1024,512]{2,1,0:T(8,128)(2,1)}, u32[]{:S(2)}) copy-start(bf16[1,1024,512]{2,1,0:T(8,128)(2,1)} %param.16) | copy-start | bytes 3145732
  5.9 0.9 %copy-start.4 = (bf16[1,16,8192]{2,1,0:T(8,128)(2,1)S(1)}, bf16[1,16,8192]{2,1,0:T(8,128)(2,1)}, u32[]{:S(2)}) copy-start(bf16[1,16,8192]{2,1,0:T(8,128)(2,1)} %param.17) | copy-start | bytes 786436
  6.9 0.9 %copy-start.5 = (bf16[128,512]{1,0:T(8,128)(2,1)S(1)}, bf16[128,512]{1,0:T(8,128)(2,1)}, u32[]{:S(2)}) copy-start(bf16[128,512]{1,0:T(8,128)(2,1)} %k_hbm.1) | copy-start | bytes 393220
  7.8 0.7 copy-start.6
  8.4 68.5 %copy-start.7 = (f32[1024,128]{1,0:T(8,128)S(1)}, f32[1024,128]{1,0:T(8,128)}, u32[]{:S(2)}) copy-start(f32[1024,128]{1,0:T(8,128)} %param.18) | copy-start | bytes 1572868
  8.4 68.5 %copy-start.8 = (f32[1024,128]{1,0:T(8,128)S(1)}, f32[1024,128]{1,0:T(8,128)}, u32[]{:S(2)}) copy-start(f32[1024,128]{1,0:T(8,128)} %param.19) | copy-start | bytes 1572868
  76.9 1.2 %copy-start.9 = (f32[4,1024]{1,0:T(4,128)S(1)}, f32[4,1024]{1,0:T(4,128)}, u32[]{:S(2)}) copy-start(f32[4,1024]{1,0:T(4,128)} %param.20) | copy-start | bytes 49156
  76.9 1.1 %copy-start.10 = (f32[4,1024]{1,0:T(4,128)S(1)}, f32[4,1024]{1,0:T(4,128)}, u32[]{:S(2)}) copy-start(f32[4,1024]{1,0:T(4,128)} %param.21) | copy-start | bytes 49156

commit v3 on v2

--- a/solution.py
+++ b/solution.py
@@ -90,6 +90,7 @@
 
 CHUNKS = 4
 EARLY = 2
+STEPS = 32767.0
 
 
 def remote(src, dst, send_sem, recv_sem, where):
@@ -101,6 +102,14 @@
         device_id=where,
         device_id_type=pl.DeviceIdType.MESH,
     )
+
+
+def to_code(scaled):
+    return jnp.floor(scaled + 0.5).astype(jnp.int32).astype(jnp.int16)
+
+
+def from_code(code):
+    return code.astype(jnp.int32).astype(jnp.float32)
 
 
 def attend(q_v, k_v, og_v):
@@ -206,9 +215,8 @@
     for p in mates:
         v_copy(f, p, v_ss.at[p]).start()
     v_copy(f, sibling, v_ss.at[sibling]).start()
-    for k in range(EARLY, CHUNKS):
-        for p in peers:
-            x_copy(k, p).start()
+    for p in peers:
+        x_copy(EARLY, p).start()
 
     loads[3].wait()
     widened = x_v[...].astype(jnp.float32)
@@ -260,10 +268,19 @@
         rows = pl.ds(pl.multiple_of(k * chunk, 128), chunk)
         return remote(g_send.at[p, rows], g_buf.at[slot, rows], g_ss.at[k, p], g_rs.at[k, slot], {"island": p})
 
+    tile = (8, 128)
+    tile_row = lax.broadcasted_iota(jnp.int32, tile, 0)
+
     def step(k, carry):
-        wv_square, gain_square = carry
+        wv_square, gain_square, levels = carry
         for p in peers:
             x_wait(k, p)
+
+        @pl.when(k + EARLY + 1 < CHUNKS)
+        def _():
+            for p in peers:
+                x_copy(k + EARLY + 1, p).start()
+
         rows = pl.ds(pl.multiple_of(k * chunk, 128), chunk)
         weight = wv_v[rows, :]
         gain = gain_ref[:, pl.ds(pl.multiple_of(f * cols + k * chunk, 128), chunk)]
@@ -291,10 +308,12 @@
             lax.dot_general(normed[...], values_all, (((0,), (0,)), ((), ())), preferred_element_type=jnp.float32)
             * scale
         )
+        level = jnp.max(jnp.max(jnp.abs(grad), axis=0, keepdims=True), axis=1, keepdims=True) + 1e-30
+        coded = grad * (STEPS / level)
         for j in range(ni):
             piece = grad[:, j * share : (j + 1) * share]
             g_own[j, rows, :] = piece
-            g_send[j, rows, :] = piece.astype(jnp.bfloat16)
+            g_send[j, rows, :] = to_code(coded[:, j * share : (j + 1) * share])
             own = slice(j * gain_share, (j + 1) * gain_share)
             gg_send[j, 0:gain_share, rows] = gain[own].astype(jnp.float32)
             gg_send[j, gain_share : 2 * gain_share, rows] = gain_grad[own]
@@ -303,13 +322,17 @@
         return (
             wv_square + jnp.sum(grad * grad, axis=0, keepdims=True),
             gain_square + jnp.sum(gain_grad * gain_grad, axis=0, keepdims=True),
+            jnp.where(tile_row == k + 2, jnp.broadcast_to(level, tile), levels),
         )
 
-    start = (jnp.zeros((1, kv_width), jnp.float32), jnp.zeros((1, chunk), jnp.float32))
-    wv_square, gain_square = lax.fori_loop(0, CHUNKS, step, start)
-
-    tile = (8, 128)
-    first = lax.broadcasted_iota(jnp.int32, tile, 0) == 0
+    start = (
+        jnp.zeros((1, kv_width), jnp.float32),
+        jnp.zeros((1, chunk), jnp.float32),
+        jnp.zeros(tile, jnp.float32),
+    )
+    wv_square, gain_square, levels = lax.fori_loop(0, CHUNKS, step, start)
+
+    first = tile_row == 0
     sq_buf[f] = jnp.where(
         first,
         jnp.broadcast_to(jnp.sum(wv_square, axis=1, keepdims=True), tile),
@@ -330,7 +353,8 @@
         sq_copy(p, p).wait_recv()
     norm = jnp.sqrt(jnp.sum(sq_buf[...], axis=0))
     bound = jnp.where(first, CLIP_SHARE * (width * kv_width) ** 0.5, CLIP_SHARE * (langs * width) ** 0.5)
-    clip_buf[i] = jnp.minimum(1.0, bound.astype(jnp.float32) / norm)
+    clip = jnp.minimum(1.0, bound.astype(jnp.float32) / norm)
+    clip_buf[i] = jnp.where(tile_row < 2, clip, clip[0:1] * levels * (1.0 / STEPS))
 
     def c_copy(slot, p):
         return remote(clip_buf.at[slot], clip_buf.at[slot], c_ss.at[p], c_rs.at[slot], {"island": p})
@@ -357,8 +381,13 @@
     tot_gain[...] = total
     total = wv_v[:, pl.ds(pl.multiple_of(i * share, 128), share)].astype(jnp.float32) - mine[0:1] * g_own[i]
     for p in zpeers:
-        total = total + lw_buf[p].astype(jnp.float32) - clip_buf[p][0:1] * g_buf[p].astype(jnp.float32)
-    tot_wv[...] = total
+        total = total + lw_buf[p].astype(jnp.float32)
+    for k in range(CHUNKS):
+        rows = slice(k * chunk, (k + 1) * chunk)
+        part = total[rows]
+        for p in zpeers:
+            part = part - clip_buf[p][k + 2 : k + 3] * from_code(g_buf[p, rows])
+        tot_wv[rows, :] = part
 
     for p in peers:
         for k in range(CHUNKS):
@@ -407,8 +436,8 @@
             vmem(langs, nf * tokens),
             vmem(nf * tokens, chunk),
             vmem(ni, cols, share, dtype=f32),
-            vmem(ni, cols, share),
-            vmem(ni, cols, share),
+            vmem(ni, cols, share, dtype=jnp.int16),
+            vmem(ni, cols, share, dtype=jnp.int16),
             vmem(ni, cols, share),
             vmem(ni, 2 * gain_share, cols, dtype=f32),
             vmem(ni, 2 * gain_share, cols, dtype=f32),
@@ -435,7 +464,7 @@
             dma((ni,)),
         ],
         compiler_params=pltpu.CompilerParams(
-            collective_id=0, has_side_effects=True, vmem_limit_bytes=48 * 1024 * 1024
+            collective_id=0, has_side_effects=True, vmem_limit_bytes=60 * 1024 * 1024
         ),
     )(block_input, lang_ids[None, :], queries, saved_keys, out_grad, local_wv[0], local_gain[0])
 

time: 79 us -> 68.3 us (0.86)
  local copies, waits for them, and re-layouts: 7.78 us -> 0.03 us
  Pallas kernels: 68.5 us -> 64.6 us
  other arithmetic: 1.73 us -> 2.77 us
    unnamed x22 -> x10, local copies, waits for them, and re-layouts: 7.78 us -> 0.03 us
    pallas_call x1, Pallas kernels: 68.5 us -> 64.6 us  [totals_by_kernel(): pl.pallas_call(functools.partial(kernel, nf, ni), out_shape=(jax.ShapeDty...]
    sub x1, other arithmetic: 1.11 us -> 2.15 us  [body(): result_wv = outer_wv - OUTER_RATE * (delta_wv + MOMENTUM * momentum_wv)]
where the time goes in v3:
time: 68.3 us; the launch traced here: 68.1 us
  Pallas kernels  64.6 us (95%)
  other arithmetic  2.77 us (4%)
  between operations  0.7 us (1%)
    pallas_call x1, Pallas kernels, totals_by_kernel(): pl.pallas_call(functools.partial(kernel, nf, ni), out_shape=(jax.ShapeDty...  64.6 us
    sub x1, other arithmetic, body(): result_wv = outer_wv - OUTER_RATE * (delta_wv + MOMENTUM * momentum_wv)  2.15 us

profile of v3, /device:TPU:0, one launch (start us, length us, event | category | flops | bytes accessed | tf_op | source)
XLA Modules:
  0.0 68.1 jit_solution(1780862060761924516)
XLA Ops:
  0.6 0.0 copy-start
  0.6 0.0 copy-start.1
  0.7 64.6 %shard_map.138 = (f32[1024,128]{1,0:T(8,128)}, f32[4,1024]{1,0:T(4,128)}) custom-call(bf16[128,8192]{1,0:T(8,128)(2,1)} %x_hbm.1, s32[1,128]{1,0:T(1,128)} %bitcast.5, bf16[128,4096]{1,0:T(8,128)(2,1)} %q_hbm.1, bf16[128,512]{1,0:T(8,128)(2,1)} %k_hbm.1, bf16[128,4096]{1,0:T(8,128)(2,1)} %og_hbm.1, bf16[1024,512]{1,0:T(8,128)(2,1)} %bitcast.3, ...), custom_call_target="tpu_custom_call" | custom-call | tf_op jit(solution)/shard_map/pallas_call | solution.py:420
  65.3 0.0 copy-start.2
  65.3 0.0 copy-start.3
  65.3 0.0 copy-start.4
  65.3 0.0 copy-done
  65.3 0.0 copy-done.1
  65.3 2.1 %multiply_subtract_fusion = (f32[1024,128]{1,0:T(8,128)}, f32[1024,128]{1,0:T(8,128)}) fusion(f32[1024,128]{1,0:T(8,128)S(1)} %copy-done, f32[1024,128]{1,0:T(8,128)} %get-tuple-element.6, f32[1024,128]{1,0:T(8,128)S(1)} %copy-done.1), kind=kLoop, calls=%fused_computation | loop fusion | flops 1048576 | bytes 2621440 | tf_op jit(solution)/shard_map/sub | solution.py:500
  67.5 0.0 copy-done.2
  67.5 0.0 copy-done.3
  67.5 0.0 copy-done.4
  67.5 0.6 multiply_subtract_fusion.2
Async XLA Ops:
  0.6 64.7 %copy-start = (f32[1024,128]{1,0:T(8,128)S(1)}, f32[1024,128]{1,0:T(8,128)}, u32[]{:S(2)}) copy-start(f32[1024,128]{1,0:T(8,128)} %param.18) | copy-start | bytes 1572868
  0.6 64.7 %copy-start.1 = (f32[1024,128]{1,0:T(8,128)S(1)}, f32[1024,128]{1,0:T(8,128)}, u32[]{:S(2)}) copy-start(f32[1024,128]{1,0:T(8,128)} %param.19) | copy-start | bytes 1572868
  65.3 2.2 %copy-start.2 = (f32[4,1024]{1,0:T(4,128)S(1)}, f32[4,1024]{1,0:T(4,128)}, u32[]{:S(2)}) copy-start(f32[4,1024]{1,0:T(4,128)} %param.20) | copy-start | bytes 49156
  65.3 2.2 %copy-start.3 = (f32[4,1024]{1,0:T(4,128)S(1)}, f32[4,1024]{1,0:T(4,128)}, u32[]{:S(2)}) copy-start(f32[4,1024]{1,0:T(4,128)} %param.21) | copy-start | bytes 49156
  65.3 2.2 %copy-start.4 = (f32[4,1024]{1,0:T(4,128)S(1)}, f32[4,1024]{1,0:T(4,128)}, u32[]{:S(2)}) copy-start(f32[4,1024]{1,0:T(4,128)} %get-tuple-element.7) | copy-start | bytes 49156

commit v4 on v3

--- a/solution.py
+++ b/solution.py
@@ -140,8 +140,8 @@
     x_hbm, lang_ref, q_hbm, k_hbm, og_hbm, wv_hbm, gain_ref,
     tot_wv, tot_gain,
     x_v, q_v, k_v, og_v, wv_v, x_buf, v_buf, s_buf, mean_b, rstd_b, hot, normed,
-    g_own, g_send, g_buf, lw_buf, gg_send, gg_buf, sq_buf, clip_buf,
-    load_sem, own_sem, x_ss, x_rs, lw_ss, lw_rs, v_ss, v_rs, fw_ss, s_ss, s_rs,
+    g_own, g_send, g_buf, lw_buf, rl_buf, pk_send, pk_buf, levels_v, gg_send, gg_buf, sq_buf, clip_buf,
+    load_sem, own_sem, x_ss, x_rs, lw_ss, lw_rs, rl_ss, rl_rs, pk_ss, pk_rs, v_ss, v_rs, fw_ss, s_ss, s_rs,
     g_ss, g_rs, gg_ss, gg_rs, sq_ss, sq_rs, c_ss, c_rs,
 ):
     f = lax.axis_index("fsdp")
@@ -198,12 +198,44 @@
         for p in peers:
             x_copy(k, p).start()
 
+    half = ni // 2
+    side = i // half
+    base, far = side * half, (1 - side) * half
+    relay, far_relay = half - 1 + side, half - side
+    near = [base + lax.rem(i - base + d, half) for d in range(1, half)]
+
+    def share_of(p):
+        return pl.ds(pl.multiple_of(p * share, 128), share)
+
     def lw_copy(p, slot):
-        src = wv_hbm.at[:, pl.ds(pl.multiple_of(p * share, 128), share)]
-        return remote(src, lw_buf.at[slot], lw_ss.at[p], lw_rs.at[slot], {"island": p})
-
-    for p in zpeers:
-        lw_copy(p, i).start()
+        return remote(wv_hbm.at[:, share_of(p)], lw_buf.at[slot], lw_ss.at[p], lw_rs.at[slot], {"island": p})
+
+    def rl_copy(e, slot, where):
+        return remote(
+            wv_hbm.at[:, share_of(far + e)], rl_buf.at[slot, e], rl_ss.at[e], rl_rs.at[slot, e], {"island": where}
+        )
+
+    def pk_copy(e):
+        return remote(pk_send.at[e], pk_buf, pk_ss.at[e], pk_rs.at[0], {"island": far + e})
+
+    def pack(e):
+        @pl.when(i == relay)
+        def _():
+            total = wv_v[:, share_of(far + e)].astype(jnp.float32)
+            for p in near:
+                rl_copy(e, p, p).wait_recv()
+                total = total + rl_buf[p, e].astype(jnp.float32)
+            level = jnp.max(jnp.max(jnp.abs(total), axis=0, keepdims=True), axis=1, keepdims=True) + 1e-30
+            pk_send[e] = to_code(total * (STEPS / level))
+            levels_v[6 + e : 7 + e, :] = jnp.broadcast_to(level * (1.0 / STEPS), (1, 128))
+            pk_copy(e).start()
+
+    levels_v[...] = jnp.zeros_like(levels_v)
+
+    @pl.when(i != relay)
+    def _():
+        for e in range(half):
+            rl_copy(e, i, relay).start()
 
     for copy in loads[:3]:
         copy.wait()
@@ -217,6 +249,8 @@
     v_copy(f, sibling, v_ss.at[sibling]).start()
     for p in peers:
         x_copy(EARLY, p).start()
+    for p in near:
+        lw_copy(p, i).start()
 
     loads[3].wait()
     widened = x_v[...].astype(jnp.float32)
@@ -242,11 +276,14 @@
 
     for p in peers:
         s_copy(f, p).start()
+    loads[4].wait()
+    pack(0)
     for p in mates:
         v_copy(p, p, v_ss.at[p]).wait_recv()
         v_copy(p, sibling, fw_ss.at[p]).start()
-
-    loads[4].wait()
+    for e in range(1, half):
+        pack(e)
+
     for copy in own_copies:
         copy.wait()
     for p in peers:
@@ -354,20 +391,20 @@
     norm = jnp.sqrt(jnp.sum(sq_buf[...], axis=0))
     bound = jnp.where(first, CLIP_SHARE * (width * kv_width) ** 0.5, CLIP_SHARE * (langs * width) ** 0.5)
     clip = jnp.minimum(1.0, bound.astype(jnp.float32) / norm)
-    clip_buf[i] = jnp.where(tile_row < 2, clip, clip[0:1] * levels * (1.0 / STEPS))
+    coded_clip = clip[0:1] * levels * (1.0 / STEPS)
+    clip_buf[i] = jnp.where(tile_row < 2, clip, jnp.where(tile_row < CHUNKS + 2, coded_clip, levels_v[...]))
 
     def c_copy(slot, p):
         return remote(clip_buf.at[slot], clip_buf.at[slot], c_ss.at[p], c_rs.at[slot], {"island": p})
 
     for p in zpeers:
         c_copy(i, p).start()
+    for p in near:
+        lw_copy(p, p).wait_recv()
     for p in zpeers:
-        lw_copy(p, p).wait_recv()
         gg_copy(p, p).wait_recv()
         c_copy(p, p).wait_recv()
-    for k in range(CHUNKS):
-        for p in zpeers:
-            g_copy(k, p, p).wait_recv()
+    remote(pk_send.at[0], pk_buf, pk_ss.at[0], pk_rs.at[0], {"island": far_relay}).wait_recv()
 
     def wide(row, size):
         return jnp.concatenate([row] * (size // 128), axis=1)
@@ -380,12 +417,15 @@
         total = total + theirs[0:gain_share] - wide(clip_buf[p][1:2], cols) * theirs[gain_share : 2 * gain_share]
     tot_gain[...] = total
     total = wv_v[:, pl.ds(pl.multiple_of(i * share, 128), share)].astype(jnp.float32) - mine[0:1] * g_own[i]
-    for p in zpeers:
+    for p in near:
         total = total + lw_buf[p].astype(jnp.float32)
+    far_levels = clip_buf[far_relay]
+    total = total + jnp.where(i == base, far_levels[6:7], far_levels[7:8]) * from_code(pk_buf[...])
     for k in range(CHUNKS):
         rows = slice(k * chunk, (k + 1) * chunk)
         part = total[rows]
         for p in zpeers:
+            g_copy(k, p, p).wait_recv()
             part = part - clip_buf[p][k + 2 : k + 3] * from_code(g_buf[p, rows])
         tot_wv[rows, :] = part
 
@@ -398,8 +438,20 @@
         v_copy(f, p, v_ss.at[p]).wait_send()
         v_copy(p, sibling, fw_ss.at[p]).wait_send()
     v_copy(f, sibling, v_ss.at[sibling]).wait_send()
+    for p in near:
+        lw_copy(p, i).wait_send()
+
+    @pl.when(i != relay)
+    def _():
+        for e in range(half):
+            rl_copy(e, i, relay).wait_send()
+
+    @pl.when(i == relay)
+    def _():
+        for e in range(half):
+            pk_copy(e).wait_send()
+
     for p in zpeers:
-        lw_copy(p, i).wait_send()
         gg_copy(p, i).wait_send()
         c_copy(i, p).wait_send()
         for k in range(CHUNKS):
@@ -439,6 +491,10 @@
             vmem(ni, cols, share, dtype=jnp.int16),
             vmem(ni, cols, share, dtype=jnp.int16),
             vmem(ni, cols, share),
+            vmem(ni, ni // 2, cols, share),
+            vmem(ni // 2, cols, share, dtype=jnp.int16),
+            vmem(cols, share, dtype=jnp.int16),
+            vmem(8, 128, dtype=f32),
             vmem(ni, 2 * gain_share, cols, dtype=f32),
             vmem(ni, 2 * gain_share, cols, dtype=f32),
             vmem(nf, 8, 128, dtype=f32),
@@ -449,6 +505,10 @@
             dma((CHUNKS, nf)),
             dma((ni,)),
             dma((ni,)),
+            dma((ni // 2,)),
+            dma((ni, ni // 2)),
+            dma((ni // 2,)),
+            dma((1,)),
             dma((nf,)),
             dma((nf,)),
             dma((nf,)),
@@ -490,6 +550,7 @@
         and block_input.shape[1] % (128 * CHUNKS * fsdp_count) == 0
         and block_input.shape[0] == 128
         and fsdp_count % 2 == 0
+        and island_count in (2, 4)
     )
     totals = totals_by_kernel if whole_tiles else totals_by_collectives
     total_wv, total_gain = totals(

time: 68.3 us -> 68.6 us (level)
  no operation moved by 1% of the time
where the time goes in v4:
time: 68.6 us; the launch traced here: 68.4 us
  Pallas kernels  64.9 us (95%)
  other arithmetic  2.77 us (4%)
  between operations  0.7 us (1%)
    pallas_call x1, Pallas kernels, totals_by_kernel(): pl.pallas_call(functools.partial(kernel, nf, ni), out_shape=(jax.ShapeDty...  64.9 us
    sub x1, other arithmetic, body(): result_wv = outer_wv - OUTER_RATE * (delta_wv + MOMENTUM * momentum_wv)  2.15 us

profile of v4, /device:TPU:0, one launch (start us, length us, event | category | flops | bytes accessed | tf_op | source)
XLA Modules:
  0.0 68.4 jit_solution(2898358967911626603)
XLA Ops:
  0.6 0.0 copy-start
  0.6 0.0 copy-start.1
  0.7 64.9 %shard_map.138 = (f32[1024,128]{1,0:T(8,128)}, f32[4,1024]{1,0:T(4,128)}) custom-call(bf16[128,8192]{1,0:T(8,128)(2,1)} %x_hbm.1, s32[1,128]{1,0:T(1,128)} %bitcast.5, bf16[128,4096]{1,0:T(8,128)(2,1)} %q_hbm.1, bf16[128,512]{1,0:T(8,128)(2,1)} %k_hbm.1, bf16[128,4096]{1,0:T(8,128)(2,1)} %og_hbm.1, bf16[1024,512]{1,0:T(8,128)(2,1)} %bitcast.3, ...), custom_call_target="tpu_custom_call" | custom-call | tf_op jit(solution)/shard_map/pallas_call | solution.py:472
  65.6 0.0 copy-start.2
  65.6 0.0 copy-start.3
  65.6 0.0 copy-start.4
  65.6 0.0 copy-done
  65.6 0.0 copy-done.1
  65.7 2.1 %multiply_subtract_fusion = (f32[1024,128]{1,0:T(8,128)}, f32[1024,128]{1,0:T(8,128)}) fusion(f32[1024,128]{1,0:T(8,128)S(1)} %copy-done, f32[1024,128]{1,0:T(8,128)} %get-tuple-element.6, f32[1024,128]{1,0:T(8,128)S(1)} %copy-done.1), kind=kLoop, calls=%fused_computation | loop fusion | flops 1048576 | bytes 2621440 | tf_op jit(solution)/shard_map/sub | solution.py:561
  67.8 0.0 copy-done.2
  67.8 0.0 copy-done.3
  67.8 0.0 copy-done.4
  67.8 0.6 multiply_subtract_fusion.2
Async XLA Ops:
  0.6 65.0 %copy-start = (f32[1024,128]{1,0:T(8,128)S(1)}, f32[1024,128]{1,0:T(8,128)}, u32[]{:S(2)}) copy-start(f32[1024,128]{1,0:T(8,128)} %param.18) | copy-start | bytes 1572868
  0.6 65.0 %copy-start.1 = (f32[1024,128]{1,0:T(8,128)S(1)}, f32[1024,128]{1,0:T(8,128)}, u32[]{:S(2)}) copy-start(f32[1024,128]{1,0:T(8,128)} %param.19) | copy-start | bytes 1572868
  65.6 2.2 %copy-start.2 = (f32[4,1024]{1,0:T(4,128)S(1)}, f32[4,1024]{1,0:T(4,128)}, u32[]{:S(2)}) copy-start(f32[4,1024]{1,0:T(4,128)} %param.20) | copy-start | bytes 49156
  65.6 2.2 %copy-start.3 = (f32[4,1024]{1,0:T(4,128)S(1)}, f32[4,1024]{1,0:T(4,128)}, u32[]{:S(2)}) copy-start(f32[4,1024]{1,0:T(4,128)} %param.21) | copy-start | bytes 49156
  65.6 2.2 %copy-start.4 = (f32[4,1024]{1,0:T(4,128)S(1)}, f32[4,1024]{1,0:T(4,128)}, u32[]{:S(2)}) copy-start(f32[4,1024]{1,0:T(4,128)} %get-tuple-element.7) | copy-start | bytes 49156

commit v5 on v4

--- a/solution.py
+++ b/solution.py
@@ -139,7 +139,7 @@
     nf, ni,
     x_hbm, lang_ref, q_hbm, k_hbm, og_hbm, wv_hbm, gain_ref,
     tot_wv, tot_gain,
-    x_v, q_v, k_v, og_v, wv_v, x_buf, v_buf, s_buf, mean_b, rstd_b, hot, normed,
+    x_v, q_v, k_v, og_v, wv_v, x_buf, v_buf, s_buf, mean_b, rstd_b, hot, normed, wide_b, split_b,
     g_own, g_send, g_buf, lw_buf, rl_buf, pk_send, pk_buf, levels_v, gg_send, gg_buf, sq_buf, clip_buf,
     load_sem, own_sem, x_ss, x_rs, lw_ss, lw_rs, rl_ss, rl_rs, pk_ss, pk_rs, v_ss, v_rs, fw_ss, s_ss, s_rs,
     g_ss, g_rs, gg_ss, gg_rs, sq_ss, sq_rs, c_ss, c_rs,
@@ -281,6 +281,9 @@
     for p in mates:
         v_copy(p, p, v_ss.at[p]).wait_recv()
         v_copy(p, sibling, fw_ss.at[p]).start()
+    for k in range(EARLY + 1, CHUNKS):
+        for p in peers:
+            x_copy(k, p).start()
     for e in range(1, half):
         pack(e)
 
@@ -312,16 +315,11 @@
         wv_square, gain_square, levels = carry
         for p in peers:
             x_wait(k, p)
-
-        @pl.when(k + EARLY + 1 < CHUNKS)
-        def _():
-            for p in peers:
-                x_copy(k + EARLY + 1, p).start()
-
         rows = pl.ds(pl.multiple_of(k * chunk, 128), chunk)
         weight = wv_v[rows, :]
         gain = gain_ref[:, pl.ds(pl.multiple_of(f * cols + k * chunk, 128), chunk)]
-        gain_grad = jnp.zeros((langs, chunk), jnp.float32)
+        values_all = v_buf[...].reshape(nf * tokens, kv_width)
+        wide_b[...] = lax.dot_general(values_all, weight, (((1,), (1,)), ((), ())), preferred_element_type=jnp.float32)
         for s in range(nf):
             at = slice(s * tokens, (s + 1) * tokens)
             mean = jnp.concatenate([mean_b[at, :]] * (chunk // tokens), axis=1)
@@ -330,17 +328,13 @@
             standard = (x_buf[k, s].astype(jnp.float32) - mean) * rstd
             gain_rows = lax.dot_general(table, gain, (((0,), (0,)), ((), ())), preferred_element_type=jnp.float32)
             normed[at, :] = (standard * gain_rows).astype(jnp.bfloat16)
-            input_grad = (
-                lax.dot_general(v_buf[s], weight, (((1,), (1,)), ((), ())), preferred_element_type=jnp.float32) * scale
-            )
-            product = standard * input_grad
+            product = standard * (wide_b[at, :] * scale)
             high = product.astype(jnp.bfloat16)
-            rest = product - high.astype(jnp.float32)
-            middle = rest.astype(jnp.bfloat16)
-            low = (rest - middle.astype(jnp.float32)).astype(jnp.bfloat16)
-            for piece in (high, middle, low):
-                gain_grad = gain_grad + jnp.dot(table, piece, preferred_element_type=jnp.float32)
-        values_all = v_buf[...].reshape(nf * tokens, kv_width)
+            split_b[0, at, :] = high
+            split_b[1, at, :] = (product - high.astype(jnp.float32)).astype(jnp.bfloat16)
+        gain_grad = jnp.dot(hot[...], split_b[0], preferred_element_type=jnp.float32) + jnp.dot(
+            hot[...], split_b[1], preferred_element_type=jnp.float32
+        )
         grad = (
             lax.dot_general(normed[...], values_all, (((0,), (0,)), ((), ())), preferred_element_type=jnp.float32)
             * scale
@@ -487,6 +481,8 @@
             vmem(nf * tokens, tokens, dtype=f32),
             vmem(langs, nf * tokens),
             vmem(nf * tokens, chunk),
+            vmem(nf * tokens, chunk, dtype=f32),
+            vmem(2, nf * tokens, chunk),
             vmem(ni, cols, share, dtype=f32),
             vmem(ni, cols, share, dtype=jnp.int16),
             vmem(ni, cols, share, dtype=jnp.int16),

time: 68.6 us -> 68.9 us (level)
  no operation moved by 1% of the time
where the time goes in v5:
time: 68.9 us; the launch traced here: 68.8 us
  Pallas kernels  65.3 us (95%)
  other arithmetic  2.77 us (4%)
  between operations  0.7 us (1%)
    pallas_call x1, Pallas kernels, totals_by_kernel(): pl.pallas_call(functools.partial(kernel, nf, ni), out_shape=(jax.ShapeDty...  65.3 us
    sub x1, other arithmetic, body(): result_wv = outer_wv - OUTER_RATE * (delta_wv + MOMENTUM * momentum_wv)  2.15 us

profile of v5, /device:TPU:0, one launch (start us, length us, event | category | flops | bytes accessed | tf_op | source)
XLA Modules:
  0.0 68.8 jit_solution(291277154516814799)
XLA Ops:
  0.6 0.0 copy-start
  0.6 0.0 copy-start.1
  0.7 65.3 %shard_map.138 = (f32[1024,128]{1,0:T(8,128)}, f32[4,1024]{1,0:T(4,128)}) custom-call(bf16[128,8192]{1,0:T(8,128)(2,1)} %x_hbm.1, s32[1,128]{1,0:T(1,128)} %bitcast.5, bf16[128,4096]{1,0:T(8,128)(2,1)} %q_hbm.1, bf16[128,512]{1,0:T(8,128)(2,1)} %k_hbm.1, bf16[128,4096]{1,0:T(8,128)(2,1)} %og_hbm.1, bf16[1024,512]{1,0:T(8,128)(2,1)} %bitcast.3, ...), custom_call_target="tpu_custom_call" | custom-call | tf_op jit(solution)/shard_map/pallas_call | solution.py:466
  65.9 0.0 copy-start.2
  65.9 0.0 copy-start.3
  66.0 0.0 copy-start.4
  66.0 0.0 copy-done
  66.0 0.0 copy-done.1
  66.0 2.1 %multiply_subtract_fusion = (f32[1024,128]{1,0:T(8,128)}, f32[1024,128]{1,0:T(8,128)}) fusion(f32[1024,128]{1,0:T(8,128)S(1)} %copy-done, f32[1024,128]{1,0:T(8,128)} %get-tuple-element.6, f32[1024,128]{1,0:T(8,128)S(1)} %copy-done.1), kind=kLoop, calls=%fused_computation | loop fusion | flops 1048576 | bytes 2621440 | tf_op jit(solution)/shard_map/sub | solution.py:557
  68.1 0.0 copy-done.2
  68.1 0.0 copy-done.3
  68.1 0.0 copy-done.4
  68.1 0.6 multiply_subtract_fusion.2
Async XLA Ops:
  0.6 65.3 %copy-start = (f32[1024,128]{1,0:T(8,128)S(1)}, f32[1024,128]{1,0:T(8,128)}, u32[]{:S(2)}) copy-start(f32[1024,128]{1,0:T(8,128)} %param.18) | copy-start | bytes 1572868
  0.6 65.3 %copy-start.1 = (f32[1024,128]{1,0:T(8,128)S(1)}, f32[1024,128]{1,0:T(8,128)}, u32[]{:S(2)}) copy-start(f32[1024,128]{1,0:T(8,128)} %param.19) | copy-start | bytes 1572868
  65.9 2.2 %copy-start.2 = (f32[4,1024]{1,0:T(4,128)S(1)}, f32[4,1024]{1,0:T(4,128)}, u32[]{:S(2)}) copy-start(f32[4,1024]{1,0:T(4,128)} %param.20) | copy-start | bytes 49156
  65.9 2.2 %copy-start.3 = (f32[4,1024]{1,0:T(4,128)S(1)}, f32[4,1024]{1,0:T(4,128)}, u32[]{:S(2)}) copy-start(f32[4,1024]{1,0:T(4,128)} %param.21) | copy-start | bytes 49156
  66.0 2.2 %copy-start.4 = (f32[4,1024]{1,0:T(4,128)S(1)}, f32[4,1024]{1,0:T(4,128)}, u32[]{:S(2)}) copy-start(f32[4,1024]{1,0:T(4,128)} %get-tuple-element.7) | copy-start | bytes 49156
